TPU v7x, 256 devices: a whole 4x4x8 slice. The times are simulated.
256 devices in a mesh: ctx: 64 (over z, y, core), head: 4 (over x).
Axes of the slice: x: 4, y: 4, z: 8, core: 2. Of those that a mesh axis runs over, the one named last changes fastest.
Arguments:
- queries: bfloat16 [16384, 32, 128], P('ctx', 'head'), may hold values from -6 to 6
- keys: bfloat16 [16384, 32, 128], P('ctx', 'head'), may hold values from -6 to 6
- values: bfloat16 [16384, 32, 128], P('ctx', 'head'), may hold values from -60 to 60, as said below
- out_grad: bfloat16 [16384, 32, 128], P('ctx', 'head'), may hold values from -6 to 6
- gain: float32 [32, 128], P('head'), may hold values from 0.1 to 1.9
- starts: int32 [4], replicated, may hold values from 0 to 16000, as said below
Outputs:
- query_grad: bfloat16 [16384, 32, 128], P('ctx', 'head')
- key_grad: bfloat16 [16384, 32, 128], P('ctx', 'head')
- value_grad: bfloat16 [16384, 32, 128], P('ctx', 'head')
Inputs may be any that keep to these rules, and one draw needn't show every extreme that they name: starts rise; the first is 0; consecutive starts lie at least 384 apart. Each head's values have their own scale.
All inputs are finite; a program needn't handle non-finite values.
Results may differ from a plain program's by a relative error of at most 0.0058.
Values sent between devices are 32-bit elements; how exact they have to be, the bound alone decides.
A program may use at most 128 MiB of HBM per device.

v0:
```python
import jax
import jax.numpy as jnp
from jax import lax
from jax.sharding import PartitionSpec as P

HEADS = 32
HEAD_DIM = 128


EPSILON = 1e-06


def carried_in(part, axis, combine, identity, reverse):
    count = lax.axis_size(axis)
    place = lax.axis_index(axis)
    ahead = count - 1 - place if reverse else place
    gathered = jax.tree.map(lambda a: lax.all_gather(a, axis), part)
    state = jax.tree.map(lambda a, e: jnp.zeros_like(a) + jnp.asarray(e, a.dtype), part, identity)

    def one(lap, state):
        source = count - 1 - lap if reverse else lap
        return combine(
            state, jax.tree.map(lambda a: lax.dynamic_index_in_dim(a, source, 0, False), gathered)
        )

    return lax.fori_loop(0, ahead, one, state)


def chain_join(earlier, later):
    return (later[0] + (1.0 - later[1]) * earlier[0], jnp.maximum(earlier[1], later[1]))


def local(queries, keys, values, out_grad, gain, starts):
    f32 = jnp.float32
    bf16 = jnp.bfloat16
    count = queries.shape[0]
    lower = lax.axis_index("ctx") * count
    posits = lower + jnp.arange(count, dtype=jnp.int32)
    seg = jnp.sum((posits[:, None] >= starts[None, :]).astype(jnp.int32), axis=1) - 1
    begins = jnp.any(posits[:, None] == starts[None, :], axis=1)
    rows = jnp.arange(count, dtype=jnp.int32)
    mask = (rows[:, None] >= rows[None, :]) & (seg[:, None] == seg[None, :])
    first_col = ((seg == seg[0]) & jnp.logical_not(begins[0]))[:, None, None]
    last_col = (seg == seg[count - 1])[:, None, None]
    cut = jnp.any(begins).astype(f32)
    tail = jnp.einsum(
        "ihd,ihe->hde", keys * last_col.astype(bf16), values, preferred_element_type=f32
    )
    empty = (jnp.zeros_like(tail), jnp.zeros((), f32))
    prefix = carried_in((tail, cut), "ctx", chain_join, empty, False)[0]
    scores = jnp.einsum("ihd,jhd->hij", queries, keys, preferred_element_type=f32)
    probs = jnp.where(mask[None], scores, 0.0).astype(bf16)
    inner = jnp.einsum("hij,jhd->ihd", probs, values, preferred_element_type=f32)
    prefix_bf = prefix.astype(bf16)
    outer = jnp.einsum("ihd,hde->ihe", queries, prefix_bf, preferred_element_type=f32)
    attn = inner + jnp.where(first_col, outer, 0.0)
    scaled = gain[None] * out_grad.astype(f32)
    width = HEADS * HEAD_DIM
    squares, crossed = lax.psum(
        (jnp.sum(attn * attn, axis=(1, 2)), jnp.sum(scaled * attn, axis=(1, 2))), "head"
    )
    meansq = squares / width + EPSILON
    cross = crossed / width
    dattn = (
        lax.rsqrt(meansq)[:, None, None] * (scaled - attn * (cross / meansq)[:, None, None])
    ).astype(bf16)
    head_part = jnp.einsum(
        "ihd,ihe->hde", queries * first_col.astype(bf16), dattn, preferred_element_type=f32
    )
    later_sum = carried_in((head_part, cut), "ctx", chain_join, empty, True)[0]
    later_bf = later_sum.astype(bf16)
    dprobs = jnp.where(
        mask[None], jnp.einsum("ihe,jhe->hij", dattn, values, preferred_element_type=f32), 0.0
    ).astype(bf16)
    query_grad = jnp.einsum("hij,jhd->ihd", dprobs, keys, preferred_element_type=f32)
    query_grad = query_grad + jnp.where(
        first_col, jnp.einsum("ihe,hde->ihd", dattn, prefix_bf, preferred_element_type=f32), 0.0
    )
    key_grad = jnp.einsum("hij,ihd->jhd", dprobs, queries, preferred_element_type=f32)
    key_grad = key_grad + jnp.where(
        last_col, jnp.einsum("jhe,hde->jhd", values, later_bf, preferred_element_type=f32), 0.0
    )
    value_grad = jnp.einsum("hij,ihe->jhe", probs, dattn, preferred_element_type=f32)
    value_grad = value_grad + jnp.where(
        last_col, jnp.einsum("jhd,hde->jhe", keys, later_bf, preferred_element_type=f32), 0.0
    )
    return (query_grad.astype(bf16), key_grad.astype(bf16), value_grad.astype(bf16))


def solution(mesh):
    return jax.shard_map(
        local,
        mesh=mesh,
        in_specs=(
            P("ctx", "head", None),
            P("ctx", "head", None),
            P("ctx", "head", None),
            P("ctx", "head", None),
            P("head", None),
            P(),
        ),
        out_specs=(P("ctx", "head", None), P("ctx", "head", None), P("ctx", "head", None)),
        check_vma=False,
    )
```

profile of v0, /device:TPU:1, one launch (start us, length us, event | category | flops | bytes accessed | tf_op | source)
XLA Modules:
  0.0 636.1 jit_solution(2546901242179922424)
XLA Ops:
  8.1 1.4 compare_reduce_fusion
  10.1 1.3 fusion.32
  11.5 1.4 broadcast_multiply_fusion.1
  16.5 130.2 %all-reduce = f32[64]{0:T(128)S(1)} all-reduce(f32[64]{0:T(128)S(1)} %dynamic-update-slice), channel_id=1, replica_groups=mesh['ctx'=64,'head'=4] {'ctx'}, use_global_device_ids=true, to_apply=%add | all-reduce | flops 64 | bytes 512
  149.4 1.5 convolution_bitcast_fusion.2
  150.9 10.8 %all-gather.5.cloned.1.call-done = f32[512,128,128]{2,1,0:T(8,128)} async-done(((f32[8,128,128]{2,1,0:T(8,128)}), f32[512,128,128]{2,1,0:T(8,128)}) %all-gather.5.cloned.1.call-update) | async-done | bytes 33554448 | tf_op jit(solution)/shard_map/all_gather | solution.py:17
  161.8 2.5 while.26
  163.0 1.2 bitcast_add_fusion.4
  164.3 2.7 multiply_reduce_fusion.1
  167.0 8.4 %all-reduce.1 = (f32[256]{0:T(256)S(1)}, f32[256]{0:T(256)S(1)}) all-reduce(f32[256]{0:T(256)S(1)} %get-tuple-element.143, f32[256]{0:T(256)S(1)} %get-tuple-element.142), channel_id=1, replica_groups=mesh['ctx'=64,'head'=4] {'head'}, use_global_device_ids=true, to_apply=%region_8.9 | all-reduce | flops 512 | bytes 4096 | tf_op jit(solution)/shard_map/psum | solution.py:59
  175.4 1.5 multiply_convert_fusion
  176.9 2.2 fusion.11
  182.5 2.6 fusion.34
  185.5 284.3 %all-gather.7.cloned.1.call-done = f32[512,128,128]{2,1,0:T(8,128)} async-done(((f32[8,128,128]{2,1,0:T(8,128)}), f32[512,128,128]{2,1,0:T(8,128)}) %all-gather.7.cloned.1.call-update) | async-done | bytes 33554448 | tf_op jit(solution)/shard_map/all_gather | solution.py:17
  469.8 155.5 %while.27 = (s32[]{:T(128)}, f32[8,128,128]{2,1,0:T(8,128)S(1)}, s32[]{:T(128)}, f32[64,8,128,128]{3,2,1,0:T(8,128)}, f32[64]{0:T(128)S(1)}, /*index=5*/s32[]{:T(128)}, s32[]{:T(128)}, s32[]{:T(128)}, s32[]{:T(128)}, f32[1]{0:T(128)}) while((s32[]{:T(128)}, f32[8,128,128]{2,1,0:T(8,128)S(1)}, s32[]{:T(128)}, f32[64,8,128,128]{3,2,1,0:T(8,128)}, ...), condition=%wide.region_10.11_spmd, body=%wide.region_9.10_spmd.sunk | while | flops 262151 | bytes 1573051 | solution.py:26
  473.5 1.2 bitcast_add_fusion.5
  476.0 1.2 bitcast_add_fusion.5
  478.6 1.2 bitcast_add_fusion.5
  481.1 1.2 bitcast_add_fusion.5
  486.1 1.2 bitcast_add_fusion.5
  491.1 1.2 bitcast_add_fusion.5
  493.6 1.2 bitcast_add_fusion.5
  496.1 1.2 bitcast_add_fusion.5
  498.6 1.2 bitcast_add_fusion.5
  503.6 1.2 bitcast_add_fusion.5
  506.1 1.2 bitcast_add_fusion.5
  508.6 1.2 bitcast_add_fusion.5
  511.2 1.2 bitcast_add_fusion.5
  513.7 1.2 bitcast_add_fusion.5
  516.2 1.2 bitcast_add_fusion.5
  521.2 1.2 bitcast_add_fusion.5
  625.2 1.6 fusion.10
  (154 shorter events, 107.6 us)
Async XLA Ops:
  7.2 5.7 copy-start
  7.2 7.6 %copy-start.6 = (bf16[256,8,128]{2,1,0:T(8,128)(2,1)S(1)}, bf16[256,8,128]{2,1,0:T(8,128)(2,1)}, u32[]{:S(2)}) copy-start(bf16[256,8,128]{2,1,0:T(8,128)(2,1)} %param.13) | copy-start | bytes 1572868
  7.2 154.5 %all-gather.5.cloned.1.call-start = ((), (), s32[]{:S(2)}) async-start(), calls=%async_computation | async-start | bytes 34078720 | tf_op jit(solution)/shard_map/all_gather | solution.py:17
  11.4 3.7 copy-start.8
  11.4 135.4 %copy-start.1 = (bf16[256,8,128]{2,1,0:T(8,128)(2,1)S(1)}, bf16[256,8,128]{2,1,0:T(8,128)(2,1)}, u32[]{:S(2)}) copy-start(bf16[256,8,128]{2,1,0:T(8,128)(2,1)} %param.10) | copy-start | bytes 1572868
  12.9 135.1 %copy-start.2 = (bf16[256,8,128]{2,1,0:T(8,128)(2,1)S(1)}, bf16[256,8,128]{2,1,0:T(8,128)(2,1)}, u32[]{:S(2)}) copy-start(bf16[256,8,128]{2,1,0:T(8,128)(2,1)} %param.11) | copy-start | bytes 1572868
  14.1 455.6 %all-gather.7.cloned.1.call-start = ((), (), s32[]{:S(2)}) async-start(), calls=%async_computation.1 | async-start | bytes 34078720 | tf_op jit(solution)/shard_map/all_gather | solution.py:17
  148.5 1.0 copy-start.3
  161.8 2.5 copy-start.7
  179.6 1.0 copy-start.4
  182.5 2.6 copy-start.5
Sparse Core Ops, SparseCore 0:
  14.2 147.4 all-gather.4
  179.3 290.4 all-gather.6
where the time goes:
time: 641 us; the launch traced here: 636 us
  waiting for transfers between devices  295 us (46%)
  blocking collectives  139 us (22%)
  other arithmetic  86.2 us (13%)
  local copies, waits for them, and re-layouts  44.5 us (7%)
  loops' own time  42.5 us (7%)
  between operations  14.9 us (2%)
  matrix products  14.1 us (2%)
    all_gather x2, waiting for transfers between devices, carried_in(): gathered = jax.tree.map(lambda a: lax.all_gather(a, axis), part)  295 us
    unnamed x1, blocking collectives  130 us
    add x63, other arithmetic, chain_join(): later[0] + (1.0 - later[1]) * earlier[0]  78.5 us
    another operation x2, loops' own time, carried_in(): return lax.fori_loop(0, ahead, one, state)  42.5 us
    dynamic_slice x63, local copies, waits for them, and re-layouts, one(): lax.dynamic_index_in_dim(a, source, 0, False)  37 us
  transfers between devices with their start and end apart: 2, of which 2 were waited for; matrix products, arithmetic and copies ran while one was open for 2% of the time, Pallas kernels for 0%

commit v1 on v0

v1 whole, which is shorter than its diff:
```python
import functools

import jax
import jax.numpy as jnp
from jax import lax
from jax.experimental import pallas as pl
from jax.experimental.pallas import tpu as pltpu
from jax.sharding import PartitionSpec as P

HEADS = 32
HEAD_DIM = 128
EPSILON = 1e-06
ZS, YS, XS = 8, 4, 4
CHIPS = ZS * YS
TOK = 256
LH = 8
HALF = 4
ROWS = HALF * HEAD_DIM
SL = ROWS // CHIPS
MESH = pl.DeviceIdType.MESH
f32 = jnp.float32
bf16 = jnp.bfloat16


def nt(a, b):
    return lax.dot_general(a, b, (((1,), (1,)), ((), ())), preferred_element_type=f32)


def nn(a, b):
    return lax.dot_general(a, b, (((1,), (0,)), ((), ())), preferred_element_type=f32)


def tn(a, b):
    return lax.dot_general(a, b, (((0,), (0,)), ((), ())), preferred_element_type=f32)


def kernel(
    starts, gain, q_in, k_in, v_in, g_in, oq, ok, ov,
    raw, tmp, qh, kh, vh, sc, mask, mask_t, first_m, last_m, probs_t, inner, attn, dat, dps, dqp, dkp, dvp,
    tme, toth, tsib, pbuf, fr, pb, sbuf, snd, stb, state, xb,
    in_sem, pair_s, pair_r, fwd_s, fwd_r, ret_s, ret_r, back_s, back_r, x_s, x_r,
):
    b = lax.axis_index("ctx")
    x = lax.axis_index("head")
    c = lax.rem(b, 2)
    m = b // 2
    oc = 1 - c
    sib = {"ctx": m * 2 + oc, "head": x}

    def chip(t):
        return {"ctx": t * 2 + c, "head": x}

    loads = [
        pltpu.make_async_copy(src, raw.at[n], in_sem.at[n])
        for n, src in enumerate((k_in, v_in, q_in, g_in))
    ]
    for load in loads:
        load.start()

    bar = pltpu.get_barrier_semaphore()
    pl.semaphore_signal(bar, inc=1, device_id=sib, device_id_type=MESH)
    for d in range(1, XS):
        pl.semaphore_signal(
            bar, inc=1, device_id={"ctx": b, "head": lax.rem(x + d, XS)}, device_id_type=MESH
        )

    @pl.loop(1, CHIPS)
    def _(d):
        pl.semaphore_signal(bar, inc=1, device_id=chip(lax.rem(m + d, CHIPS)), device_id_type=MESH)

    st = [starts[n] for n in range(4)]

    def seg_of(pos):
        total = (pos >= st[0]).astype(jnp.int32)
        for n in range(1, 4):
            total = total + (pos >= st[n]).astype(jnp.int32)
        return total

    def keep(lo, size):
        hit = (st[0] >= lo) & (st[0] < lo + size)
        for n in range(1, 4):
            hit = hit | ((st[n] >= lo) & (st[n] < lo + size))
        return jnp.where(hit, 0.0, 1.0).astype(f32)

    base = b * TOK
    row_c = lax.broadcasted_iota(jnp.int32, (TOK, HEAD_DIM), 0) + base
    seg_c = seg_of(row_c)
    begins0 = (base == st[0]) | (base == st[1]) | (base == st[2]) | (base == st[3])
    seg0 = jnp.where(begins0, -1, seg_of(base))
    first_m[...] = (seg_c == seg0).astype(f32)
    last_m[...] = (seg_c == seg_of(base + TOK - 1)).astype(f32)

    def relayout(n, out):
        tmp[...] = raw[n].astype(f32).reshape(TOK * LH, HEAD_DIM)
        for h in range(LH):
            out[h] = tmp[pl.ds(h, TOK, stride=LH), :].astype(out.dtype)

    loads[0].wait()
    relayout(0, kh)
    loads[1].wait()
    relayout(1, vh)

    def tail_of(h):
        return tn((kh[h].astype(f32) * last_m[...]).astype(bf16), vh[h])

    def pair_copy(src, dst, ss, rs):
        return pltpu.make_async_remote_copy(
            src_ref=src, dst_ref=dst, send_sem=ss, recv_sem=rs, device_id=sib, device_id_type=MESH
        )

    for r in range(HALF):
        toth[0, r * HEAD_DIM : (r + 1) * HEAD_DIM] = tail_of(oc * HALF + r)
    pl.semaphore_wait(bar, CHIPS + XS - 1)

    def scan(s, make_mine, w_me, w_sib, middle, reverse):
        first_pair = pair_copy(toth.at[s], tsib.at[s], pair_s.at[s], pair_r.at[s])
        first_pair.start()
        make_mine()
        first_pair.wait()
        pbuf[s] = tme[s] * w_me + tsib[s] * w_sib
        fr[s, pl.ds(m, 1)] = pbuf[s, pl.ds(pl.multiple_of(m * SL, SL), SL)][None]

        @pl.loop(1, CHIPS)
        def _(d):
            t = lax.rem(m + d, CHIPS)
            pltpu.make_async_remote_copy(
                src_ref=pbuf.at[s, pl.ds(pl.multiple_of(t * SL, SL), SL)],
                dst_ref=fr.at[s, m],
                send_sem=fwd_s.at[s],
                recv_sem=fwd_r.at[s],
                device_id=chip(t),
                device_id_type=MESH,
            ).start()

        middle()
        others = pl.ds(0, CHIPS - 1)
        whole = pltpu.make_async_copy(fr.at[s, others], fr.at[s, others], fwd_r.at[s])
        whole.wait()

        def step(n, carry):
            t = CHIPS - 1 - n if reverse else n
            pb[s, pl.ds(t, 1)] = carry[None]
            return fr[s, t] + keep(t * 2 * TOK, 2 * TOK) * carry

        lax.fori_loop(0, CHIPS, step, jnp.zeros((SL, HEAD_DIM), f32), unroll=True)
        sbuf[s, pl.ds(m, 1)] = pb[s, pl.ds(m, 1)]

        @pl.loop(1, CHIPS)
        def _(d):
            t = lax.rem(m + d, CHIPS)
            pltpu.make_async_remote_copy(
                src_ref=pb.at[s, t],
                dst_ref=sbuf.at[s, m],
                send_sem=ret_s.at[s],
                recv_sem=ret_r.at[s],
                device_id=chip(t),
                device_id_type=MESH,
            ).start()

        whole = pltpu.make_async_copy(sbuf.at[s, others], sbuf.at[s, others], ret_r.at[s])
        whole.wait()
        edge = 1 if reverse else 0
        whole_state = sbuf[s].reshape(ROWS, HEAD_DIM)
        is_edge = c == edge
        inner_part = jnp.where(is_edge, tme[s], tsib[s])
        away = inner_part + keep((2 * m + edge) * TOK, TOK) * whole_state
        snd[s] = jnp.where(is_edge, away, whole_state)
        back = pair_copy(snd.at[s], stb.at[s], back_s.at[s], back_r.at[s])
        back.start()
        mine = jnp.where(is_edge, whole_state, away).astype(bf16)
        state[s, pl.ds(c * HALF, HALF)] = mine.reshape(HALF, HEAD_DIM, HEAD_DIM)
        back.wait()
        state[s, pl.ds(oc * HALF, HALF)] = stb[s].astype(bf16).reshape(HALF, HEAD_DIM, HEAD_DIM)
        sent = pltpu.make_async_copy(fr.at[s, others], fr.at[s, others], fwd_s.at[s])
        sent.wait()
        sent = pltpu.make_async_copy(sbuf.at[s, others], sbuf.at[s, others], ret_s.at[s])
        sent.wait()

    def my_tails():
        for r in range(HALF):
            tme[0, r * HEAD_DIM : (r + 1) * HEAD_DIM] = tail_of(c * HALF + r)

    def middle_fwd():
        loads[2].wait()
        relayout(2, qh)
        loads[3].wait()
        relayout(3, sc)
        ri = lax.broadcasted_iota(jnp.int32, (TOK, TOK), 0)
        ci = lax.broadcasted_iota(jnp.int32, (TOK, TOK), 1)
        same = seg_of(ri + base) == seg_of(ci + base)
        mask[...] = ((ri >= ci) & same).astype(f32)
        mask_t[...] = ((ri <= ci) & same).astype(f32)

        @pl.loop(0, LH)
        def _(h):
            sc[h] = sc[h] * gain[pl.ds(h, 1), :]
            p = (nt(qh[h], kh[h]) * mask[...]).astype(bf16)
            probs_t[h] = (nt(kh[h], qh[h]) * mask_t[...]).astype(bf16)
            inner[h] = nn(p, vh[h])

    keep_even = keep(2 * m * TOK, TOK)
    keep_odd = keep((2 * m + 1) * TOK, TOK)
    one = jnp.ones((), f32)
    scan(
        0,
        my_tails,
        jnp.where(c == 0, keep_odd, one),
        jnp.where(c == 0, one, keep_odd),
        middle_fwd,
        False,
    )

    def attn_step(h, sums):
        a = inner[h] + first_m[...] * nn(qh[h], state[0, h])
        attn[h] = a
        return sums[0] + a * a, sums[1] + a * sc[h]

    zero = jnp.zeros((TOK, HEAD_DIM), f32)
    sq, cr = lax.fori_loop(0, LH, attn_step, (zero, zero))
    sq_row = jnp.sum(sq.T, axis=0, keepdims=True)
    cr_row = jnp.sum(cr.T, axis=0, keepdims=True)
    which = lax.broadcasted_iota(jnp.int32, (8, TOK), 0)
    xb[pl.ds(x, 1)] = jnp.where(which == 0, sq_row, cr_row)[None]
    for d in range(1, XS):
        pltpu.make_async_remote_copy(
            src_ref=xb.at[x],
            dst_ref=xb.at[x],
            send_sem=x_s,
            recv_sem=x_r,
            device_id={"ctx": b, "head": lax.rem(x + d, XS)},
            device_id_type=MESH,
        ).start()
    pltpu.make_async_copy(xb.at[pl.ds(0, XS - 1)], xb.at[pl.ds(0, XS - 1)], x_r).wait()
    tot = xb[0] + xb[1] + xb[2] + xb[3]
    width = HEADS * HEAD_DIM
    meansq = tot[0:1] / width + EPSILON
    cross = tot[1:2] / width
    rr = jnp.broadcast_to(lax.rsqrt(meansq), (HEAD_DIM, TOK)).T
    co = jnp.broadcast_to(cross / meansq, (HEAD_DIM, TOK)).T

    @pl.loop(0, LH)
    def _(h):
        dat[h] = (rr * (sc[h] - attn[h] * co)).astype(bf16)

    def head_of(h):
        return tn((qh[h].astype(f32) * first_m[...]).astype(bf16), dat[h])

    for r in range(HALF):
        toth[1, r * HEAD_DIM : (r + 1) * HEAD_DIM] = head_of(oc * HALF + r)

    def my_heads():
        for r in range(HALF):
            tme[1, r * HEAD_DIM : (r + 1) * HEAD_DIM] = head_of(c * HALF + r)

    def middle_bwd():
        for h in range(LH):
            dp = (nt(dat[h], vh[h]) * mask[...]).astype(bf16)
            dpt = (nt(vh[h], dat[h]) * mask_t[...]).astype(bf16)
            dq = nn(dp, kh[h]) + first_m[...] * nt(dat[h], state[0, h])
            tmp[pl.ds(h, TOK, stride=LH), :] = dq
            dkp[h] = nn(dpt, qh[h])
            dvp[h] = nn(probs_t[h], dat[h])
        oq[...] = tmp[...].reshape(TOK, LH, HEAD_DIM).astype(bf16)

    scan(
        1,
        my_heads,
        jnp.where(c == 1, keep_even, one),
        jnp.where(c == 1, one, keep_even),
        middle_bwd,
        True,
    )
    for h in range(LH):
        tmp[pl.ds(h, TOK, stride=LH), :] = dkp[h] + last_m[...] * nt(vh[h], state[1, h])
    ok[...] = tmp[...].reshape(TOK, LH, HEAD_DIM).astype(bf16)
    for h in range(LH):
        tmp[pl.ds(h, TOK, stride=LH), :] = dvp[h] + last_m[...] * nn(kh[h], state[1, h])
    ov[...] = tmp[...].reshape(TOK, LH, HEAD_DIM).astype(bf16)
    pltpu.make_async_copy(xb.at[pl.ds(0, XS - 1)], xb.at[pl.ds(0, XS - 1)], x_s).wait()


def local(queries, keys, values, out_grad, gain, starts):
    vm = pl.BlockSpec(memory_space=pltpu.VMEM)
    hb = pl.BlockSpec(memory_space=pl.ANY)
    out = jax.ShapeDtypeStruct((TOK, LH, HEAD_DIM), bf16)
    V = pltpu.VMEM
    D = pltpu.SemaphoreType.DMA
    return pl.pallas_call(
        kernel,
        out_shape=(out, out, out),
        in_specs=[pl.BlockSpec(memory_space=pltpu.SMEM), vm, hb, hb, hb, hb],
        out_specs=(vm, vm, vm),
        scratch_shapes=[
            V((4, TOK, LH, HEAD_DIM), bf16),
            V((TOK * LH, HEAD_DIM), f32),
            V((LH, TOK, HEAD_DIM), bf16),
            V((LH, TOK, HEAD_DIM), bf16),
            V((LH, TOK, HEAD_DIM), bf16),
            V((LH, TOK, HEAD_DIM), f32),
            V((TOK, TOK), f32),
            V((TOK, TOK), f32),
            V((TOK, HEAD_DIM), f32),
            V((TOK, HEAD_DIM), f32),
            V((LH, TOK, TOK), bf16),
            V((LH, TOK, HEAD_DIM), f32),
            V((LH, TOK, HEAD_DIM), f32),
            V((LH, TOK, HEAD_DIM), bf16),
            V((8, HEAD_DIM), f32),
            V((8, HEAD_DIM), f32),
            V((LH, TOK, HEAD_DIM), f32),
            V((LH, TOK, HEAD_DIM), f32),
            V((2, ROWS, HEAD_DIM), f32),
            V((2, ROWS, HEAD_DIM), f32),
            V((2, ROWS, HEAD_DIM), f32),
            V((2, ROWS, HEAD_DIM), f32),
            V((2, CHIPS, SL, HEAD_DIM), f32),
            V((2, CHIPS, SL, HEAD_DIM), f32),
            V((2, CHIPS, SL, HEAD_DIM), f32),
            V((2, ROWS, HEAD_DIM), f32),
            V((2, ROWS, HEAD_DIM), f32),
            V((2, LH, HEAD_DIM, HEAD_DIM), bf16),
            V((XS, 8, TOK), f32),
            D((4,)),
            D((2,)),
            D((2,)),
            D((2,)),
            D((2,)),
            D((2,)),
            D((2,)),
            D((2,)),
            D((2,)),
            D,
            D,
        ],
        compiler_params=pltpu.CompilerParams(
            collective_id=0, has_side_effects=True, vmem_limit_bytes=48 * 2**20
        ),
        cost_estimate=pl.CostEstimate(
            flops=1_400_000_000, bytes_accessed=4_000_000, transcendentals=2048
        ),
        name="fused",
    )(starts, gain, queries, keys, values, out_grad)


def solution(mesh):
    spec = P("ctx", "head", None)
    return jax.shard_map(
        local,
        mesh=mesh,
        in_specs=(spec, spec, spec, spec, P("head", None), P()),
        out_specs=(spec, spec, spec),
        check_vma=False,
    )
```

time: 641 us -> 71.3 us (0.11)
  waiting for transfers between devices: 295 us -> 0 us
  blocking collectives: 139 us -> 0 us
  other arithmetic: 86.2 us -> 0 us
  Pallas kernels: 0 us -> 62.5 us
  loops' own time: 42.5 us -> 0 us
  local copies, waits for them, and re-layouts: 44.5 us -> 7.88 us
  between operations: 14.9 us -> 0.65 us
  matrix products: 14.1 us -> 0 us
    all_gather x2 -> x0, waiting for transfers between devices: 295 us -> none  [carried_in(): gathered = jax.tree.map(lambda a: lax.all_gather(a, axis), part)]
    unnamed x1 -> x0, blocking collectives: 130 us -> none
    add x64 -> x0, other arithmetic: 78.5 us -> none  [the longest x63 78.5 us: chain_join(): later[0] + (1.0 - later[1]) * earlier[0]]
    pallas_call x0 -> x1, Pallas kernels: none -> 62.5 us  [local(): pl.pallas_call(kernel, out_shape=(out, out, out), in_specs=[pl.BlockSpec(...]
    another operation x2 -> x0, loops' own time: 42.5 us -> none  [carried_in(): return lax.fori_loop(0, ahead, one, state)]
    dynamic_slice x63 -> x0, local copies, waits for them, and re-layouts: 37 us -> none  [one(): lax.dynamic_index_in_dim(a, source, 0, False)]
    dot_general x12 -> x0, matrix products: 14.1 us -> none  [the longest x1 2.72 us: local(): jnp.einsum('ihd,hde->ihe', queries, prefix_bf, preferred_element_type=f32)]
    psum x1 -> x0, blocking collectives: 8.39 us -> none  [local(): lax.psum((jnp.sum(attn * attn, axis=(1, 2)), jnp.sum(scaled * attn, axis=...]
  transfers between devices with their start and end apart: 2 -> 0, of which waited for: 2 -> 0; matrix products, arithmetic and copies ran while one was open for 2% -> 0% of each run, Pallas kernels for 0% -> 0%
where the time goes in v1:
time: 71.3 us; the launch traced here: 71 us
  Pallas kernels  62.5 us (88%)
  local copies, waits for them, and re-layouts  7.88 us (11%)
    pallas_call x1, Pallas kernels, local(): pl.pallas_call(kernel, out_shape=(out, out, out), in_specs=[pl.BlockSpec(...  62.5 us
    unnamed x15, local copies, waits for them, and re-layouts  7.88 us

profile of v1, /device:TPU:1, one launch (start us, length us, event | category | flops | bytes accessed | tf_op | source)
XLA Modules:
  0.0 71.0 jit_solution(3733421295710742188)
XLA Ops:
  0.6 0.0 copy-start
  0.6 1.0 %copy-done = bf16[256,8,128]{2,1,0:T(8,128)(2,1)S(1)} copy-done((bf16[256,8,128]{2,1,0:T(8,128)(2,1)S(1)}, bf16[256,8,128]{2,1,0:T(8,128)(2,1)}, u32[]{:S(2)}) %copy-start) | copy-done | bytes 524312
  1.7 0.0 copy-start.1
  1.7 1.0 %copy-done.1 = bf16[256,8,128]{2,1,0:T(8,128)(2,1)S(1)} copy-done((bf16[256,8,128]{2,1,0:T(8,128)(2,1)S(1)}, bf16[256,8,128]{2,1,0:T(8,128)(2,1)}, u32[]{:S(2)}) %copy-start.1) | copy-done | bytes 524312
  2.7 0.0 copy-start.2
  2.7 1.0 %copy-done.2 = bf16[256,8,128]{2,1,0:T(8,128)(2,1)S(1)} copy-done((bf16[256,8,128]{2,1,0:T(8,128)(2,1)S(1)}, bf16[256,8,128]{2,1,0:T(8,128)(2,1)}, u32[]{:S(2)}) %copy-start.2) | copy-done | bytes 524312
  3.8 0.0 copy-start.3
  3.8 1.0 %copy-done.3 = bf16[256,8,128]{2,1,0:T(8,128)(2,1)S(1)} copy-done((bf16[256,8,128]{2,1,0:T(8,128)(2,1)S(1)}, bf16[256,8,128]{2,1,0:T(8,128)(2,1)}, u32[]{:S(2)}) %copy-start.3) | copy-done | bytes 524312
  4.8 0.0 copy-start.4
  4.8 0.7 copy-done.4
  5.5 0.0 copy-start.5
  5.5 0.7 copy-done.5
  6.1 62.5 %fused.1 = (bf16[256,8,128]{2,1,0:T(8,128)(2,1)S(1)}, bf16[256,8,128]{2,1,0:T(8,128)(2,1)S(1)}, bf16[256,8,128]{2,1,0:T(8,128)(2,1)S(1)}) custom-call(s32[4]{0:T(128)S(1)} %copy-done.5, f32[8,128]{1,0:T(8,128)S(1)} %copy-done.4, bf16[256,8,128]{2,1,0:T(8,128)(2,1)S(1)} %copy-done, bf16[256,8,128]{2,1,0:T(8,128)(2,1)S(1)} %copy-done.1, ...), custom_call_target="tpu_custom_call" | custom-call | flops 1400000000 | bytes 4000000 | tf_op jit(solution)/shard_map/fused/pallas_call | solution.py:288
  68.6 0.8 %copy.12 = bf16[256,8,128]{2,1,0:T(8,128)(2,1)} copy(bf16[256,8,128]{2,1,0:T(8,128)(2,1)S(1)} %get-tuple-element.6) | data formatting | bytes 1048576
  69.4 0.8 %copy.13 = bf16[256,8,128]{2,1,0:T(8,128)(2,1)} copy(bf16[256,8,128]{2,1,0:T(8,128)(2,1)S(1)} %get-tuple-element.7) | data formatting | bytes 1048576
  70.2 0.8 %copy.14 = bf16[256,8,128]{2,1,0:T(8,128)(2,1)} copy(bf16[256,8,128]{2,1,0:T(8,128)(2,1)S(1)} %get-tuple-element.8) | data formatting | bytes 1048576
Async XLA Ops:
  0.6 1.0 %copy-start = (bf16[256,8,128]{2,1,0:T(8,128)(2,1)S(1)}, bf16[256,8,128]{2,1,0:T(8,128)(2,1)}, u32[]{:S(2)}) copy-start(bf16[256,8,128]{2,1,0:T(8,128)(2,1)} %q_in.1) | copy-start | bytes 1572868
  1.7 1.0 %copy-start.1 = (bf16[256,8,128]{2,1,0:T(8,128)(2,1)S(1)}, bf16[256,8,128]{2,1,0:T(8,128)(2,1)}, u32[]{:S(2)}) copy-start(bf16[256,8,128]{2,1,0:T(8,128)(2,1)} %k_in.1) | copy-start | bytes 1572868
  2.7 1.0 %copy-start.2 = (bf16[256,8,128]{2,1,0:T(8,128)(2,1)S(1)}, bf16[256,8,128]{2,1,0:T(8,128)(2,1)}, u32[]{:S(2)}) copy-start(bf16[256,8,128]{2,1,0:T(8,128)(2,1)} %v_in.1) | copy-start | bytes 1572868
  3.8 1.0 %copy-start.3 = (bf16[256,8,128]{2,1,0:T(8,128)(2,1)S(1)}, bf16[256,8,128]{2,1,0:T(8,128)(2,1)}, u32[]{:S(2)}) copy-start(bf16[256,8,128]{2,1,0:T(8,128)(2,1)} %g_in.1) | copy-start | bytes 1572868
  4.8 0.7 copy-start.4
  5.5 0.7 copy-start.5

commit v2 on v1

v2 whole, which is shorter than its diff:
```python
import jax
import jax.numpy as jnp
from jax import lax
from jax.experimental import pallas as pl
from jax.experimental.pallas import tpu as pltpu
from jax.sharding import PartitionSpec as P

HEADS = 32
HEAD_DIM = 128
EPSILON = 1e-06
ZS, YS, XS = 8, 4, 4
CHIPS = ZS * YS
TOK = 256
LH = 8
HALF = 4
GROUPS = 2
GH = HALF // GROUPS
ROWS = GH * HEAD_DIM
SL = ROWS // CHIPS
CHUNK = 64
PIECES = 4
MESH = pl.DeviceIdType.MESH
f32 = jnp.float32
bf16 = jnp.bfloat16


def nt(a, b):
    return lax.dot_general(a, b, (((1,), (1,)), ((), ())), preferred_element_type=f32)


def nn(a, b):
    return lax.dot_general(a, b, (((1,), (0,)), ((), ())), preferred_element_type=f32)


def tn(a, b):
    return lax.dot_general(a, b, (((0,), (0,)), ((), ())), preferred_element_type=f32)


def kernel(
    starts_in, gain_in, q_in, k_in, v_in, g_in, oq, tk, tv,
    starts, gain, raw, tmp, qh, kh, vh, sc, mask, mask_t, first_m, last_m, qft, probs_t, inner, attn, dat, dkp, dvp,
    sqp, crp, rr, co, keeps, tme, toth, tsib, pbuf, fr, pb, sbuf, snd, stb, state, xb,
    in_sem, pair_s, pair_r, fwd_s, fwd_r, ret_s, ret_r, back_s, back_r, x_s, x_r,
):
    b = lax.axis_index("ctx")
    x = lax.axis_index("head")
    c = lax.rem(b, 2)
    m = b // 2
    mz = m // YS
    my = lax.rem(m, YS)
    oc = 1 - c
    sib = {"ctx": m * 2 + oc, "head": x}

    def chip(t):
        return {"ctx": t * 2 + c, "head": x}

    loads = [
        pltpu.make_async_copy(src, dst, in_sem.at[n])
        for n, (src, dst) in enumerate(
            (
                (starts_in, starts),
                (k_in, raw.at[0]),
                (v_in, raw.at[1]),
                (q_in, raw.at[2]),
                (g_in, raw.at[3]),
                (gain_in, gain),
            )
        )
    ]
    for load in loads:
        load.start()

    bar = pltpu.get_barrier_semaphore()
    pl.semaphore_signal(bar, inc=1, device_id=sib, device_id_type=MESH)
    for d in range(1, XS):
        pl.semaphore_signal(
            bar, inc=1, device_id={"ctx": b, "head": lax.rem(x + d, XS)}, device_id_type=MESH
        )

    def far_first(n):
        i = n // YS
        j = lax.rem(n, YS)
        dz = ZS // 2 + (1 - 2 * lax.rem(i, 2)) * ((i + 1) // 2)
        dy = YS // 2 + (1 - 2 * lax.rem(j, 2)) * ((j + 1) // 2)
        return lax.rem(mz + dz, ZS) * YS + lax.rem(my + dy, YS)

    @pl.loop(0, CHIPS - 1)
    def _(n):
        pl.semaphore_signal(bar, inc=1, device_id=chip(far_first(n)), device_id_type=MESH)

    loads[0].wait()
    st = [starts[n] for n in range(4)]

    def seg_of(pos):
        total = (pos >= st[0]).astype(jnp.int32)
        for n in range(1, 4):
            total = total + (pos >= st[n]).astype(jnp.int32)
        return total

    def keep(lo, size):
        hit = (st[0] >= lo) & (st[0] < lo + size)
        for n in range(1, 4):
            hit = hit | ((st[n] >= lo) & (st[n] < lo + size))
        return jnp.where(hit, 0.0, 1.0).astype(f32)

    base = b * TOK
    row_c = lax.broadcasted_iota(jnp.int32, (TOK, HEAD_DIM), 0) + base
    seg_c = seg_of(row_c)
    begins0 = (base == st[0]) | (base == st[1]) | (base == st[2]) | (base == st[3])
    seg0 = jnp.where(begins0, -1, seg_of(base))
    first_m[...] = (seg_c == seg0).astype(f32)
    last_m[...] = (seg_c == seg_of(base + TOK - 1)).astype(f32)

    def relayout(n, out, tmp):
        tmp[...] = raw[n].astype(f32).reshape(TOK * LH, HEAD_DIM)
        for h in range(LH):
            out[h] = tmp[pl.ds(h, TOK, stride=LH), :].astype(out.dtype)

    loads[1].wait()
    relayout(0, kh, tk)
    loads[2].wait()
    relayout(1, vh, tv)

    def tail_of(h):
        return tn((kh[h].astype(f32) * last_m[...]).astype(bf16), vh[h])

    def head_of(h):
        return nn(qft[h], dat[h])

    def pair_copy(src, dst, ss, rs):
        return pltpu.make_async_remote_copy(
            src_ref=src, dst_ref=dst, send_sem=ss, recv_sem=rs, device_id=sib, device_id_type=MESH
        )

    def to_all(src_of, dst, ss, rs):
        @pl.loop(0, CHIPS - 1)
        def _(n):
            t = far_first(n)
            pltpu.make_async_remote_copy(
                src_ref=src_of(t),
                dst_ref=dst.at[m],
                send_sem=ss,
                recv_sem=rs,
                device_id=chip(t),
                device_id_type=MESH,
            ).start()

    def bytes_of_others(buf, sem):
        part = buf.at[pl.ds(0, CHIPS - 1)]
        pltpu.make_async_copy(part, part, sem).wait()

    def sums(s, g, part_of):
        for r in range(GH):
            toth[s * GROUPS + g, r * HEAD_DIM : (r + 1) * HEAD_DIM] = part_of(oc * HALF + g * GH + r)

    def scan(s, part_of, w_me, w_sib, middle, late, use, reverse):
        at = [s * GROUPS + g for g in range(GROUPS)]
        firsts = [
            pair_copy(toth.at[i], tsib.at[i], pair_s.at[i], pair_r.at[i]) for i in at
        ]
        for g, i in enumerate(at):
            sums(s, g, part_of)
            if s == 0 and g == 0:
                pl.semaphore_wait(bar, CHIPS + XS - 1)
            firsts[g].start()
        for g, i in enumerate(at):
            for r in range(GH):
                tme[i, r * HEAD_DIM : (r + 1) * HEAD_DIM] = part_of(c * HALF + g * GH + r)
            firsts[g].wait_recv()
            pbuf[i] = (tme[i] * w_me + tsib[i] * w_sib).reshape(CHIPS, SL, HEAD_DIM)
            to_all(lambda t, i=i: pbuf.at[i, t], fr.at[i], fwd_s.at[i], fwd_r.at[i])
            fr[i, pl.ds(m, 1)] = pbuf[i, pl.ds(m, 1)]
        middle()
        for i in at:
            bytes_of_others(fr.at[i], fwd_r.at[i])
            carry = jnp.zeros((SL, HEAD_DIM), f32)
            for n in range(CHIPS):
                t = CHIPS - 1 - n if reverse else n
                pb[i, t] = carry
                carry = fr[i, t] + keeps[t] * carry
            to_all(lambda t, i=i: pb.at[i, t], sbuf.at[i], ret_s.at[i], ret_r.at[i])
            sbuf[i, pl.ds(m, 1)] = pb[i, pl.ds(m, 1)]
        late()
        edge = 1 if reverse else 0
        is_edge = c == edge
        edge_keep = keep((2 * m + edge) * TOK, TOK)
        backs = [pair_copy(snd.at[i], stb.at[i], back_s.at[i], back_r.at[i]) for i in at]
        for g, i in enumerate(at):
            bytes_of_others(sbuf.at[i], ret_r.at[i])
            whole = sbuf[i].reshape(ROWS, HEAD_DIM)
            away = jnp.where(is_edge, tme[i], tsib[i]) + edge_keep * whole
            snd[i] = jnp.where(is_edge, away, whole)
            backs[g].start()
            mine = jnp.where(is_edge, whole, away).astype(bf16)
            state[s, pl.ds(c * HALF + g * GH, GH)] = mine.reshape(GH, HEAD_DIM, HEAD_DIM)
        for g, i in enumerate(at):
            backs[g].wait_recv()
            theirs = stb[i].astype(bf16)
            state[s, pl.ds(oc * HALF + g * GH, GH)] = theirs.reshape(GH, HEAD_DIM, HEAD_DIM)
            use(g, [k * HALF + g * GH + r for k in range(2) for r in range(GH)])

    def near_fwd(h):
        p = (nt(qh[h], kh[h]) * mask[...]).astype(bf16)
        probs_t[h] = (nt(kh[h], qh[h]) * mask_t[...]).astype(bf16)
        inner[h] = nn(p, vh[h])
        qft[h] = (qh[h].astype(f32) * first_m[...]).T.astype(bf16)

    def middle_fwd():
        chip_row = lax.broadcasted_iota(jnp.int32, (CHIPS, SL, HEAD_DIM), 0)
        keeps[...] = keep(chip_row * (2 * TOK), 2 * TOK)
        loads[3].wait()
        relayout(2, qh, tk)
        ri = lax.broadcasted_iota(jnp.int32, (TOK, TOK), 0)
        ci = lax.broadcasted_iota(jnp.int32, (TOK, TOK), 1)
        same = seg_of(ri + base) == seg_of(ci + base)
        mask[...] = ((ri >= ci) & same).astype(f32)
        mask_t[...] = ((ri <= ci) & same).astype(f32)
        for h in range(HALF):
            near_fwd(h)

    def late_fwd():
        for h in range(HALF, LH):
            near_fwd(h)
        loads[4].wait()
        loads[5].wait()
        relayout(3, sc, tv)
        for h in range(LH):
            sc[h] = sc[h] * gain[h : h + 1, :]

    def use_fwd(g, hs):
        for lo in range(0, TOK, CHUNK):
            rows = pl.ds(lo, CHUNK)
            sq = jnp.zeros((CHUNK, HEAD_DIM), f32)
            cr = jnp.zeros((CHUNK, HEAD_DIM), f32)
            for h in hs:
                a = inner[h, rows] + first_m[rows] * nn(qh[h, rows], state[0, h])
                attn[h, rows] = a
                sq = sq + a * a
                cr = cr + a * sc[h, rows]
            sqp[g, rows] = sq
            crp[g, rows] = cr

    keep_even = keep(2 * m * TOK, TOK)
    keep_odd = keep((2 * m + 1) * TOK, TOK)
    one = jnp.ones((), f32)
    scan(
        0,
        tail_of,
        jnp.where(c == 0, keep_odd, one),
        jnp.where(c == 0, one, keep_odd),
        middle_fwd,
        late_fwd,
        use_fwd,
        False,
    )

    sq_row = jnp.sum((sqp[0] + sqp[1]).T, axis=0, keepdims=True)
    cr_row = jnp.sum((crp[0] + crp[1]).T, axis=0, keepdims=True)
    which = lax.broadcasted_iota(jnp.int32, (8, TOK), 0)
    xb[pl.ds(x, 1)] = jnp.where(which == 0, sq_row, cr_row)[None]
    for d in (2, 1, 3):
        pltpu.make_async_remote_copy(
            src_ref=xb.at[x],
            dst_ref=xb.at[x],
            send_sem=x_s,
            recv_sem=x_r,
            device_id={"ctx": b, "head": lax.rem(x + d, XS)},
            device_id_type=MESH,
        ).start()
    pltpu.make_async_copy(xb.at[pl.ds(0, XS - 1)], xb.at[pl.ds(0, XS - 1)], x_r).wait()
    tot = xb[0] + xb[1] + xb[2] + xb[3]
    width = HEADS * HEAD_DIM
    meansq = tot[0:1] / width + EPSILON
    cross = tot[1:2] / width
    rr[...] = jnp.broadcast_to(lax.rsqrt(meansq), (HEAD_DIM, TOK)).T
    co[...] = jnp.broadcast_to(cross / meansq, (HEAD_DIM, TOK)).T

    def dattn_head(h):
        dat[h] = (rr[...] * (sc[h] - attn[h] * co[...])).astype(bf16)
        return head_of(h)

    def near_bwd(h):
        dp = (nt(dat[h], vh[h]) * mask[...]).astype(bf16)
        dpt = (nt(vh[h], dat[h]) * mask_t[...]).astype(bf16)
        dq = nn(dp, kh[h]) + first_m[...] * nt(dat[h], state[0, h])
        tmp[pl.ds(h, TOK, stride=LH), :] = dq
        dkp[h] = nn(dpt, qh[h])
        dvp[h] = nn(probs_t[h], dat[h])

    def middle_bwd():
        for h in range(HALF):
            near_bwd(h)

    def late_bwd():
        for h in range(HALF, LH):
            near_bwd(h)
        oq[...] = tmp[...].reshape(TOK, LH, HEAD_DIM).astype(bf16)

    def use_bwd(g, hs):
        for h in hs:
            at = pl.ds(h, TOK, stride=LH)
            tk[at, :] = dkp[h] + last_m[...] * nt(vh[h], state[1, h])
            tv[at, :] = dvp[h] + last_m[...] * nn(kh[h], state[1, h])

    scan(
        1,
        dattn_head,
        jnp.where(c == 1, keep_even, one),
        jnp.where(c == 1, one, keep_even),
        middle_bwd,
        late_bwd,
        use_bwd,
        True,
    )
    pltpu.make_async_copy(xb.at[pl.ds(0, XS - 1)], xb.at[pl.ds(0, XS - 1)], x_s).wait()
    for i in range(2 * GROUPS):
        pair_copy(toth.at[i], tsib.at[i], pair_s.at[i], pair_r.at[i]).wait_send()
        pair_copy(snd.at[i], stb.at[i], back_s.at[i], back_r.at[i]).wait_send()
        bytes_of_others(fr.at[i], fwd_s.at[i])
        bytes_of_others(sbuf.at[i], ret_s.at[i])


def finish(oq, tk, tv, out_q, out_k, out_v, buf, sem):
    pltpu.make_async_copy(oq, out_q, sem.at[0]).start()
    for n, (src, dst) in enumerate(((tk, out_k), (tv, out_v))):
        for p in range(PIECES):
            rows = pl.ds(p * TOK // PIECES, TOK // PIECES)
            flat = pl.ds(p * TOK * LH // PIECES, TOK * LH // PIECES)
            buf[n, rows] = src[flat, :].reshape(TOK // PIECES, LH, HEAD_DIM).astype(bf16)
            pltpu.make_async_copy(buf.at[n, rows], dst.at[rows], sem.at[1 + n * PIECES + p]).start()
    pltpu.make_async_copy(oq, out_q, sem.at[0]).wait()
    for n, dst in enumerate((out_k, out_v)):
        for p in range(PIECES):
            rows = pl.ds(p * TOK // PIECES, TOK // PIECES)
            pltpu.make_async_copy(buf.at[n, rows], dst.at[rows], sem.at[1 + n * PIECES + p]).wait()


def local(queries, keys, values, out_grad, gain, starts):
    vm = pl.BlockSpec(memory_space=pltpu.VMEM)
    hb = pl.BlockSpec(memory_space=pltpu.HBM)
    args = [
        pltpu.with_memory_space_constraint(a, pltpu.HBM)
        for a in (starts, gain, queries, keys, values, out_grad)
    ]
    flat = jax.ShapeDtypeStruct((TOK * LH, HEAD_DIM), f32)
    out = jax.ShapeDtypeStruct((TOK, LH, HEAD_DIM), bf16)
    V = pltpu.VMEM
    D = pltpu.SemaphoreType.DMA
    N = 2 * GROUPS
    heads16 = V((LH, TOK, HEAD_DIM), bf16)
    heads32 = V((LH, TOK, HEAD_DIM), f32)
    cols = V((TOK, HEAD_DIM), f32)
    part = V((N, ROWS, HEAD_DIM), f32)
    slices = V((N, CHIPS, SL, HEAD_DIM), f32)
    parts = pl.pallas_call(
        kernel,
        out_shape=(out, flat, flat),
        in_specs=[hb] * 6,
        out_specs=(vm, vm, vm),
        scratch_shapes=[
            pltpu.SMEM((4,), jnp.int32),
            V((LH, HEAD_DIM), f32),
            V((4, TOK, LH, HEAD_DIM), bf16),
            V((TOK * LH, HEAD_DIM), f32),
            heads16,
            heads16,
            heads16,
            heads32,
            V((TOK, TOK), f32),
            V((TOK, TOK), f32),
            cols,
            cols,
            V((LH, HEAD_DIM, TOK), bf16),
            V((LH, TOK, TOK), bf16),
            heads32,
            heads32,
            heads16,
            heads32,
            heads32,
            V((2, TOK, HEAD_DIM), f32),
            V((2, TOK, HEAD_DIM), f32),
            cols,
            cols,
            V((CHIPS, SL, HEAD_DIM), f32),
            part,
            part,
            part,
            slices,
            slices,
            slices,
            slices,
            part,
            part,
            V((2, LH, HEAD_DIM, HEAD_DIM), bf16),
            V((XS, 8, TOK), f32),
            D((6,)),
            D((N,)),
            D((N,)),
            D((N,)),
            D((N,)),
            D((N,)),
            D((N,)),
            D((N,)),
            D((N,)),
            D,
            D,
        ],
        compiler_params=pltpu.CompilerParams(
            collective_id=0, has_side_effects=True, vmem_limit_bytes=32 * 2**20
        ),
        cost_estimate=pl.CostEstimate(
            flops=1_400_000_000, bytes_accessed=4_000_000, transcendentals=2048
        ),
        name="fused",
    )(*args)
    return pl.pallas_call(
        finish,
        out_shape=(out, out, out),
        in_specs=[vm] * 3,
        out_specs=(hb, hb, hb),
        scratch_shapes=[V((2, TOK, LH, HEAD_DIM), bf16), D((1 + 2 * PIECES,))],
        compiler_params=pltpu.CompilerParams(vmem_limit_bytes=4 * 2**20),
        name="finish",
    )(*parts)


def solution(mesh):
    spec = P("ctx", "head", None)
    return jax.shard_map(
        local,
        mesh=mesh,
        in_specs=(spec, spec, spec, spec, P("head", None), P()),
        out_specs=(spec, spec, spec),
        check_vma=False,
    )
```

time: 71.3 us -> 55.6 us (0.78)
  local copies, waits for them, and re-layouts: 7.88 us -> 0 us
  Pallas kernels: 62.5 us -> 54.9 us
    unnamed x15 -> x0, local copies, waits for them, and re-layouts: 7.88 us -> none
    pallas_call x1 -> x2, Pallas kernels: 62.5 us -> 54.9 us  [the longest x1 53.7 us: local(): pl.pallas_call(kernel, out_shape=(out, flat, flat), in_specs=[hb] * 6, ou...]
where the time goes in v2:
time: 55.6 us
  Pallas kernels  54.9 us (99%)
  between operations  0.64 us (1%)
    pallas_call x1, Pallas kernels, local(): pl.pallas_call(kernel, out_shape=(out, flat, flat), in_specs=[hb] * 6, ou...  53.7 us
    pallas_call x1, Pallas kernels, local(): pl.pallas_call(finish, out_shape=(out, out, out), in_specs=[vm] * 3, out_...  1.21 us

profile of v2, /device:TPU:1, one launch (start us, length us, event | category | flops | bytes accessed | tf_op | source)
XLA Modules:
  0.0 55.6 jit_solution(3231840500699335291)
XLA Ops:
  0.6 53.7 %fused.1 = (bf16[256,8,128]{2,1,0:T(8,128)(2,1)S(1)}, f32[2048,128]{1,0:T(8,128)S(1)}, f32[2048,128]{1,0:T(8,128)S(1)}) custom-call(s32[4]{0:T(128)} %starts_in.1, f32[8,128]{1,0:T(8,128)} %gain_in.1, bf16[256,8,128]{2,1,0:T(8,128)(2,1)} %q_in.1, bf16[256,8,128]{2,1,0:T(8,128)(2,1)} %k_in.1, bf16[256,8,128]{2,1,0:T(8,128)(2,1)} %v_in.1, ...), custom_call_target="tpu_custom_call" | custom-call | flops 1400000000 | bytes 4000000 | tf_op jit(solution)/shard_map/fused/pallas_call | solution.py:355
  54.4 1.2 %finish.1 = (bf16[256,8,128]{2,1,0:T(8,128)(2,1)}, bf16[256,8,128]{2,1,0:T(8,128)(2,1)}, bf16[256,8,128]{2,1,0:T(8,128)(2,1)}) custom-call(bf16[256,8,128]{2,1,0:T(8,128)(2,1)S(1)} %get-tuple-element.6.oq, f32[2048,128]{1,0:T(8,128)S(1)} %get-tuple-element.7.tk, f32[2048,128]{1,0:T(8,128)S(1)} %get-tuple-element.8.tv), custom_call_target="tpu_custom_call" | custom-call | tf_op jit(solution)/shard_map/finish/pallas_call | solution.py:416

commit v3 on v2

v3 whole, which is shorter than its diff:
```python
import jax
import jax.numpy as jnp
from jax import lax
from jax.experimental import pallas as pl
from jax.experimental.pallas import tpu as pltpu
from jax.sharding import PartitionSpec as P

HEADS = 32
HEAD_DIM = 128
EPSILON = 1e-06
ZS, YS, XS = 8, 4, 4
CHIPS = ZS * YS
TOK = 256
LH = 8
HALF = 4
GROUPS = 2
GH = HALF // GROUPS
ROWS = GH * HEAD_DIM
SL = ROWS // CHIPS
CHUNK = 64
PIECES = 4
FAR = sorted(
    ((dz, dy) for dz in range(ZS) for dy in range(YS) if dz or dy),
    key=lambda o: -(min(o[0], ZS - o[0]) + min(o[1], YS - o[1])),
)
MESH = pl.DeviceIdType.MESH
f32 = jnp.float32
bf16 = jnp.bfloat16


def nt(a, b):
    return lax.dot_general(a, b, (((1,), (1,)), ((), ())), preferred_element_type=f32)


def nn(a, b):
    return lax.dot_general(a, b, (((1,), (0,)), ((), ())), preferred_element_type=f32)


def tn(a, b):
    return lax.dot_general(a, b, (((0,), (0,)), ((), ())), preferred_element_type=f32)


def kernel(
    starts_in, gain_in, q_in, k_in, v_in, g_in, oq, tk, tv,
    starts, gain, raw, tmp, qh, kh, vh, sc, mask, mask_t, first_m, last_m, probs_t, dat, dkp, dvp,
    xin, xat, xsc, yin, ysc, yq, rq, yd, rd, xq, qft, st,
    sqp, crp, rr, co, keeps, tme, toth, tsib, hodd, pbuf, fr, pb, sbuf, snd, stb, xb, tot,
    in_sem, pair_s, pair_r, fwd_s, fwd_r, ret_s, ret_r, back_s, back_r, ex_s, ex_r, yd_s, yd_r, x_s, x_r,
):
    b = lax.axis_index("ctx")
    x = lax.axis_index("head")
    c = lax.rem(b, 2)
    m = b // 2
    mz = m // YS
    my = lax.rem(m, YS)
    oc = 1 - c
    sib = {"ctx": m * 2 + oc, "head": x}

    def chip(t):
        return {"ctx": t * 2 + c, "head": x}

    loads = [
        pltpu.make_async_copy(src, dst, in_sem.at[n])
        for n, (src, dst) in enumerate(
            (
                (starts_in, starts),
                (k_in, raw.at[0]),
                (v_in, raw.at[1]),
                (q_in, raw.at[2]),
                (g_in, raw.at[3]),
                (gain_in, gain),
            )
        )
    ]

    def others(n):
        return lax.rem(mz + FAR[n][0], ZS) * YS + lax.rem(my + FAR[n][1], YS)

    peers = [
        {"ctx": m * 2 + lax.rem(c + e, 2), "head": lax.rem(x + d, XS)}
        for d in (2, 1, 3, 0)
        for e in (1, 0)
        if (d, e) != (0, 0)
    ]
    bar = pltpu.get_barrier_semaphore()
    for n in range(CHIPS - 1):
        pl.semaphore_signal(bar, inc=1, device_id=chip(others(n)), device_id_type=MESH)
    for peer in peers:
        pl.semaphore_signal(bar, inc=1, device_id=peer, device_id_type=MESH)
    for load in loads:
        load.start()

    loads[0].wait()
    sv = [starts[n] for n in range(4)]

    def seg_of(pos):
        total = (pos >= sv[0]).astype(jnp.int32)
        for n in range(1, 4):
            total = total + (pos >= sv[n]).astype(jnp.int32)
        return total

    def keep(lo, size):
        hit = (sv[0] >= lo) & (sv[0] < lo + size)
        for n in range(1, 4):
            hit = hit | ((sv[n] >= lo) & (sv[n] < lo + size))
        return jnp.where(hit, 0.0, 1.0).astype(f32)

    base = b * TOK
    row_c = lax.broadcasted_iota(jnp.int32, (TOK, HEAD_DIM), 0) + base
    seg_c = seg_of(row_c)
    begins0 = (base == sv[0]) | (base == sv[1]) | (base == sv[2]) | (base == sv[3])
    seg0 = jnp.where(begins0, -1, seg_of(base))
    first_m[...] = (seg_c == seg0).astype(f32)
    last_m[...] = (seg_c == seg_of(base + TOK - 1)).astype(f32)
    keep_even = keep(2 * m * TOK, TOK)
    keep_odd = keep((2 * m + 1) * TOK, TOK)

    def relayout(n, out, tmp):
        tmp[...] = raw[n].astype(f32).reshape(TOK * LH, HEAD_DIM)
        for h in range(LH):
            out[h] = tmp[pl.ds(h, TOK, stride=LH), :].astype(out.dtype)

    def pair_copy(src, dst, ss, rs):
        return pltpu.make_async_remote_copy(
            src_ref=src, dst_ref=dst, send_sem=ss, recv_sem=rs, device_id=sib, device_id_type=MESH
        )

    def to_all(src, dst, ss, rs):
        for n in range(CHIPS - 1):
            t = others(n)
            pltpu.make_async_remote_copy(
                src_ref=src.at[t],
                dst_ref=dst.at[m],
                send_sem=ss,
                recv_sem=rs,
                device_id=chip(t),
                device_id_type=MESH,
            ).start()

    def bytes_of(buf, count, sem):
        part = buf.at[pl.ds(0, count)]
        pltpu.make_async_copy(part, part, sem).wait()

    def rows_of(r):
        return pl.ds(r * HEAD_DIM, HEAD_DIM)

    def forward(i, p):
        pbuf[i] = p.reshape(CHIPS, SL, HEAD_DIM)
        to_all(pbuf.at[i], fr.at[i], fwd_s.at[i], fwd_r.at[i])
        fr[i, pl.ds(m, 1)] = pbuf[i, pl.ds(m, 1)]

    def turn(i, reverse):
        bytes_of(fr.at[i], CHIPS - 1, fwd_r.at[i])
        carry = jnp.zeros((SL, HEAD_DIM), f32)
        for n in range(CHIPS):
            t = CHIPS - 1 - n if reverse else n
            pb[i, t] = carry
            carry = fr[i, t] + keeps[t] * carry
        to_all(pb.at[i], sbuf.at[i], ret_s.at[i], ret_r.at[i])
        sbuf[i, pl.ds(m, 1)] = pb[i, pl.ds(m, 1)]

    def split(i, edge, part, weight):
        bytes_of(sbuf.at[i], CHIPS - 1, ret_r.at[i])
        whole = sbuf[i].reshape(ROWS, HEAD_DIM)
        away = part + weight * whole
        is_edge = c == edge
        snd[i] = jnp.where(is_edge, away, whole)
        pair_copy(snd.at[i], stb.at[i], back_s.at[i], back_r.at[i]).start()
        return jnp.where(is_edge, whole, away)

    loads[1].wait()
    relayout(0, kh, tk)
    loads[2].wait()
    relayout(1, vh, tv)

    def tail_of(h):
        return tn((kh[h].astype(f32) * last_m[...]).astype(bf16), vh[h])

    for g in range(GROUPS):
        for r in range(GH):
            toth[g, rows_of(r)] = tail_of(oc * HALF + g * GH + r)
    for g in range(GROUPS):
        for r in range(GH):
            tme[g, rows_of(r)] = tail_of(c * HALF + g * GH + r)
    pl.semaphore_wait(bar, CHIPS - 1 + len(peers))
    one = jnp.ones((), f32)
    w_me = jnp.where(c == 0, keep_odd, one)
    w_sib = jnp.where(c == 0, one, keep_odd)
    firsts = [pair_copy(toth.at[g], tsib.at[g], pair_s.at[g], pair_r.at[g]) for g in range(GROUPS)]
    for g in range(GROUPS):
        firsts[g].start()
    for g in range(GROUPS):
        firsts[g].wait_recv()
        forward(g, tme[g] * w_me + tsib[g] * w_sib)

    chip_row = lax.broadcasted_iota(jnp.int32, (CHIPS, SL, HEAD_DIM), 0)
    keeps[...] = keep(chip_row * (2 * TOK), 2 * TOK)
    loads[3].wait()
    relayout(2, qh, tk)
    ri = lax.broadcasted_iota(jnp.int32, (TOK, TOK), 0)
    ci = lax.broadcasted_iota(jnp.int32, (TOK, TOK), 1)
    same = seg_of(ri + base) == seg_of(ci + base)
    mask[...] = ((ri >= ci) & same).astype(f32)
    mask_t[...] = ((ri <= ci) & same).astype(f32)

    def near_fwd(h):
        p = (nt(qh[h], kh[h]) * mask[...]).astype(bf16)
        probs_t[h] = (nt(kh[h], qh[h]) * mask_t[...]).astype(bf16)
        return nn(p, vh[h])

    swaps = [
        pair_copy(src, dst, ex_s.at[n], ex_r.at[n])
        for n, (src, dst) in enumerate(((yin, xin.at[1]), (yq, rq), (ysc, xsc.at[1])))
    ]
    for r in range(HALF):
        h = oc * HALF + r
        yq[r] = qh[h].astype(f32) * first_m[...]
        yin[r] = near_fwd(h)
    swaps[0].start()
    swaps[1].start()
    turn(0, False)
    turn(1, False)
    loads[4].wait()
    loads[5].wait()
    relayout(3, sc, tv)
    for r in range(HALF):
        ysc[r] = sc[oc * HALF + r] * gain[pl.ds(oc * HALF + r, 1), :]
    swaps[2].start()
    for r in range(HALF):
        h = c * HALF + r
        xsc[0, r] = sc[h] * gain[pl.ds(h, 1), :]
        masked = qh[h].astype(f32) * first_m[...]
        xq[0, r] = masked.astype(bf16)
        qft[0, r] = masked.T.astype(bf16)
        xin[0, r] = near_fwd(h)
    swaps[1].wait_recv()
    for r in range(HALF):
        xq[1, r] = rq[r].astype(bf16)
        qft[1, r] = rq[r].T.astype(bf16)
    swaps[0].wait_recv()
    swaps[2].wait_recv()

    for g in range(GROUPS):
        own = split(g, 0, jnp.where(c == 0, tme[g], tsib[g]), keep_even)
        st[0, g * GH : (g + 1) * GH] = own.astype(bf16).reshape(GH, HEAD_DIM, HEAD_DIM)
        st[1, g * GH : (g + 1) * GH] = snd[g].astype(bf16).reshape(GH, HEAD_DIM, HEAD_DIM)
        for j in range(2):
            for lo in range(0, TOK, CHUNK):
                rows = pl.ds(lo, CHUNK)
                sq = jnp.zeros((CHUNK, HEAD_DIM), f32)
                cr = jnp.zeros((CHUNK, HEAD_DIM), f32)
                for r in range(g * GH, (g + 1) * GH):
                    a = xin[j, r, rows] + nn(xq[j, r, rows], st[j, r])
                    xat[j, r, rows] = a
                    sq = sq + a * a
                    cr = cr + a * xsc[j, r, rows]
                sqp[g, j, rows] = sq
                crp[g, j, rows] = cr

    which = lax.broadcasted_iota(jnp.int32, (8, HEAD_DIM), 0)
    tile = jnp.zeros((8, HEAD_DIM), f32)
    for j, core in enumerate((c, oc)):
        for n, part in enumerate((sqp, crp)):
            line = jnp.sum((part[0, j] + part[1, j]).T, axis=0, keepdims=True)
            for k in range(2):
                half = line[:, k * HEAD_DIM : (k + 1) * HEAD_DIM]
                tile = jnp.where(which == n * 4 + core * 2 + k, half, tile)
    slot = x * 2 + c
    xb[pl.ds(slot, 1)] = tile[None]
    for peer in peers:
        pltpu.make_async_remote_copy(
            src_ref=xb.at[slot],
            dst_ref=xb.at[slot],
            send_sem=x_s,
            recv_sem=x_r,
            device_id=peer,
            device_id_type=MESH,
        ).start()
    bytes_of(xb, len(peers), x_r)
    total = xb[0]
    for n in range(1, 2 * XS):
        total = total + xb[n]
    width = HEADS * HEAD_DIM
    meansq = total[0:4] / width + EPSILON
    cross = total[4:8] / width
    tot[0:4] = lax.rsqrt(meansq)
    tot[4:8] = cross / meansq
    for j, core in enumerate((c, oc)):
        for k in range(2):
            rows = pl.ds(k * HEAD_DIM, HEAD_DIM)
            for n, out in enumerate((rr, co)):
                line = tot[pl.ds(n * 4 + core * 2 + k, 1), :]
                out[j, rows] = jnp.broadcast_to(line, (HEAD_DIM, HEAD_DIM)).T

    gives = [pair_copy(yd.at[g], rd.at[g], yd_s.at[g], yd_r.at[g]) for g in range(GROUPS)]
    for g in range(GROUPS):
        parts = []
        for r in range(GH):
            at = g * GH + r
            pair = []
            for j in range(2):
                d = rr[j] * (xsc[j, at] - xat[j, at] * co[j])
                d = d.astype(bf16)
                if j == 0:
                    dat[c * HALF + at] = d
                else:
                    yd[g, r] = d.astype(f32)
                pair.append(nn(qft[j, at], d))
            even = jnp.where(c == 0, pair[0], pair[1])
            odd = jnp.where(c == 0, pair[1], pair[0])
            hodd[g, rows_of(r)] = odd
            parts.append(even + keep_even * odd)
        forward(GROUPS + g, jnp.concatenate(parts, axis=0))
        gives[g].start()

    def near_bwd(h, state):
        dp = (nt(dat[h], vh[h]) * mask[...]).astype(bf16)
        dpt = (nt(vh[h], dat[h]) * mask_t[...]).astype(bf16)
        dq = nn(dp, kh[h]) + first_m[...] * nt(dat[h], state)
        tmp[pl.ds(h, TOK, stride=LH), :] = dq
        dkp[h] = nn(dpt, qh[h])
        dvp[h] = nn(probs_t[h], dat[h])

    for r in range(HALF):
        near_bwd(c * HALF + r, st[0, r])
    for g in range(GROUPS):
        turn(GROUPS + g, True)
    for g in range(GROUPS):
        pair_copy(snd.at[g], stb.at[g], back_s.at[g], back_r.at[g]).wait_recv()
        gives[g].wait_recv()
        for r in range(GH):
            h = oc * HALF + g * GH + r
            dat[h] = rd[g, r].astype(bf16)
            near_bwd(h, stb[g, rows_of(r)].astype(bf16))
    oq[...] = tmp[...].reshape(TOK, LH, HEAD_DIM).astype(bf16)

    def last_of(h, state):
        at = pl.ds(h, TOK, stride=LH)
        tk[at, :] = dkp[h] + last_m[...] * nt(vh[h], state)
        tv[at, :] = dvp[h] + last_m[...] * nn(kh[h], state)

    for g in range(GROUPS):
        own = split(GROUPS + g, 1, hodd[g], keep_odd).astype(bf16)
        for r in range(GH):
            last_of(c * HALF + g * GH + r, own[r * HEAD_DIM : (r + 1) * HEAD_DIM])
    for g in range(GROUPS):
        i = GROUPS + g
        pair_copy(snd.at[i], stb.at[i], back_s.at[i], back_r.at[i]).wait_recv()
        for r in range(GH):
            last_of(oc * HALF + g * GH + r, stb[i, rows_of(r)].astype(bf16))

    bytes_of(xb, len(peers), x_s)
    for swap in swaps:
        swap.wait_send()
    for g in range(GROUPS):
        firsts[g].wait_send()
        gives[g].wait_send()
    for i in range(2 * GROUPS):
        pair_copy(snd.at[i], stb.at[i], back_s.at[i], back_r.at[i]).wait_send()
        bytes_of(fr.at[i], CHIPS - 1, fwd_s.at[i])
        bytes_of(sbuf.at[i], CHIPS - 1, ret_s.at[i])


def finish(oq, tk, tv, out_q, out_k, out_v, buf, sem):
    pltpu.make_async_copy(oq, out_q, sem.at[0]).start()
    for n, (src, dst) in enumerate(((tk, out_k), (tv, out_v))):
        for p in range(PIECES):
            rows = pl.ds(p * TOK // PIECES, TOK // PIECES)
            flat = pl.ds(p * TOK * LH // PIECES, TOK * LH // PIECES)
            buf[n, rows] = src[flat, :].reshape(TOK // PIECES, LH, HEAD_DIM).astype(bf16)
            pltpu.make_async_copy(buf.at[n, rows], dst.at[rows], sem.at[1 + n * PIECES + p]).start()
    pltpu.make_async_copy(oq, out_q, sem.at[0]).wait()
    for n, dst in enumerate((out_k, out_v)):
        for p in range(PIECES):
            rows = pl.ds(p * TOK // PIECES, TOK // PIECES)
            pltpu.make_async_copy(buf.at[n, rows], dst.at[rows], sem.at[1 + n * PIECES + p]).wait()


def local(queries, keys, values, out_grad, gain, starts):
    vm = pl.BlockSpec(memory_space=pltpu.VMEM)
    hb = pl.BlockSpec(memory_space=pltpu.HBM)
    args = [
        pltpu.with_memory_space_constraint(a, pltpu.HBM)
        for a in (starts, gain, queries, keys, values, out_grad)
    ]
    flat = jax.ShapeDtypeStruct((TOK * LH, HEAD_DIM), f32)
    out = jax.ShapeDtypeStruct((TOK, LH, HEAD_DIM), bf16)
    V = pltpu.VMEM
    D = pltpu.SemaphoreType.DMA
    N = 2 * GROUPS
    heads16 = V((LH, TOK, HEAD_DIM), bf16)
    heads32 = V((LH, TOK, HEAD_DIM), f32)
    cols = V((TOK, HEAD_DIM), f32)
    half32 = V((HALF, TOK, HEAD_DIM), f32)
    both32 = V((2, HALF, TOK, HEAD_DIM), f32)
    part = V((GROUPS, ROWS, HEAD_DIM), f32)
    parts2 = V((N, ROWS, HEAD_DIM), f32)
    slices = V((N, CHIPS, SL, HEAD_DIM), f32)
    parts = pl.pallas_call(
        kernel,
        out_shape=(out, flat, flat),
        in_specs=[hb] * 6,
        out_specs=(vm, vm, vm),
        scratch_shapes=[
            pltpu.SMEM((4,), jnp.int32),
            V((LH, HEAD_DIM), f32),
            V((4, TOK, LH, HEAD_DIM), bf16),
            V((TOK * LH, HEAD_DIM), f32),
            heads16,
            heads16,
            heads16,
            heads32,
            V((TOK, TOK), f32),
            V((TOK, TOK), f32),
            cols,
            cols,
            V((LH, TOK, TOK), bf16),
            heads16,
            heads32,
            heads32,
            both32,
            both32,
            both32,
            half32,
            half32,
            half32,
            half32,
            V((GROUPS, GH, TOK, HEAD_DIM), f32),
            V((GROUPS, GH, TOK, HEAD_DIM), f32),
            V((2, HALF, TOK, HEAD_DIM), bf16),
            V((2, HALF, HEAD_DIM, TOK), bf16),
            V((2, HALF, HEAD_DIM, HEAD_DIM), bf16),
            V((GROUPS, 2, TOK, HEAD_DIM), f32),
            V((GROUPS, 2, TOK, HEAD_DIM), f32),
            V((2, TOK, HEAD_DIM), f32),
            V((2, TOK, HEAD_DIM), f32),
            V((CHIPS, SL, HEAD_DIM), f32),
            part,
            part,
            part,
            part,
            slices,
            slices,
            slices,
            slices,
            parts2,
            parts2,
            V((2 * XS, 8, HEAD_DIM), f32),
            V((8, HEAD_DIM), f32),
            D((6,)),
            D((GROUPS,)),
            D((GROUPS,)),
            D((N,)),
            D((N,)),
            D((N,)),
            D((N,)),
            D((N,)),
            D((N,)),
            D((3,)),
            D((3,)),
            D((GROUPS,)),
            D((GROUPS,)),
            D,
            D,
        ],
        compiler_params=pltpu.CompilerParams(
            collective_id=0, has_side_effects=True, vmem_limit_bytes=32 * 2**20
        ),
        cost_estimate=pl.CostEstimate(
            flops=1_400_000_000, bytes_accessed=4_000_000, transcendentals=2048
        ),
        name="fused",
    )(*args)
    return pl.pallas_call(
        finish,
        out_shape=(out, out, out),
        in_specs=[vm] * 3,
        out_specs=(hb, hb, hb),
        scratch_shapes=[V((2, TOK, LH, HEAD_DIM), bf16), D((1 + 2 * PIECES,))],
        compiler_params=pltpu.CompilerParams(vmem_limit_bytes=4 * 2**20),
        name="finish",
    )(*parts)


def solution(mesh):
    spec = P("ctx", "head", None)
    return jax.shard_map(
        local,
        mesh=mesh,
        in_specs=(spec, spec, spec, spec, P("head", None), P()),
        out_specs=(spec, spec, spec),
        check_vma=False,
    )
```

time: 55.6 us -> 52.2 us (0.939)
  Pallas kernels: 54.9 us -> 51.4 us
    pallas_call x1, Pallas kernels: 53.7 us -> 50.2 us  [local(): pl.pallas_call(kernel, out_shape=(out, flat, flat), in_specs=[hb] * 6, ou...]
where the time goes in v3:
time: 52.2 us; the launch traced here: 52.1 us
  Pallas kernels  51.4 us (98%)
  between operations  0.64 us (1%)
    pallas_call x1, Pallas kernels, local(): pl.pallas_call(kernel, out_shape=(out, flat, flat), in_specs=[hb] * 6, ou...  50.2 us
    pallas_call x1, Pallas kernels, local(): pl.pallas_call(finish, out_shape=(out, out, out), in_specs=[vm] * 3, out_...  1.21 us

profile of v3, /device:TPU:1, one launch (start us, length us, event | category | flops | bytes accessed | tf_op | source)
XLA Modules:
  0.0 52.1 jit_solution(15212792981753227948)
XLA Ops:
  0.6 50.2 %fused.1 = (bf16[256,8,128]{2,1,0:T(8,128)(2,1)S(1)}, f32[2048,128]{1,0:T(8,128)S(1)}, f32[2048,128]{1,0:T(8,128)S(1)}) custom-call(s32[4]{0:T(128)} %starts_in.1, f32[8,128]{1,0:T(8,128)} %gain_in.1, bf16[256,8,128]{2,1,0:T(8,128)(2,1)} %q_in.1, bf16[256,8,128]{2,1,0:T(8,128)(2,1)} %k_in.1, bf16[256,8,128]{2,1,0:T(8,128)(2,1)} %v_in.1, ...), custom_call_target="tpu_custom_call" | custom-call | flops 1400000000 | bytes 4000000 | tf_op jit(solution)/shard_map/fused/pallas_call | solution.py:399
  50.9 1.2 %finish.1 = (bf16[256,8,128]{2,1,0:T(8,128)(2,1)}, bf16[256,8,128]{2,1,0:T(8,128)(2,1)}, bf16[256,8,128]{2,1,0:T(8,128)(2,1)}) custom-call(bf16[256,8,128]{2,1,0:T(8,128)(2,1)S(1)} %get-tuple-element.6.oq, f32[2048,128]{1,0:T(8,128)S(1)} %get-tuple-element.7.tk, f32[2048,128]{1,0:T(8,128)S(1)} %get-tuple-element.8.tv), custom_call_target="tpu_custom_call" | custom-call | tf_op jit(solution)/shard_map/finish/pallas_call | solution.py:474

commit v4 on v3

--- a/solution.py
+++ b/solution.py
@@ -18,6 +18,7 @@
 ROWS = GH * HEAD_DIM
 SL = ROWS // CHIPS
 CHUNK = 64
+EARLY = 1
 PIECES = 4
 FAR = sorted(
     ((dz, dy) for dz in range(ZS) for dy in range(YS) if dz or dy),
@@ -44,8 +45,8 @@
     starts_in, gain_in, q_in, k_in, v_in, g_in, oq, tk, tv,
     starts, gain, raw, tmp, qh, kh, vh, sc, mask, mask_t, first_m, last_m, probs_t, dat, dkp, dvp,
     xin, xat, xsc, yin, ysc, yq, rq, yd, rd, xq, qft, st,
-    sqp, crp, rr, co, keeps, tme, toth, tsib, hodd, pbuf, fr, pb, sbuf, snd, stb, xb, tot,
-    in_sem, pair_s, pair_r, fwd_s, fwd_r, ret_s, ret_r, back_s, back_r, ex_s, ex_r, yd_s, yd_r, x_s, x_r,
+    sqp, crp, rr, co, keeps, tme, toth, tsib, hodd, pbuf, fr, pb, sbuf, direct, snd, stb, xb, tot,
+    in_sem, pair_s, pair_r, fwd_s, fwd_r, ret_s, ret_r, dir_s, dir_r, back_s, back_r, ex_s, ex_r, yd_s, yd_r, x_s, x_r,
 ):
     b = lax.axis_index("ctx")
     x = lax.axis_index("head")
@@ -125,17 +126,24 @@
             src_ref=src, dst_ref=dst, send_sem=ss, recv_sem=rs, device_id=sib, device_id_type=MESH
         )
 
-    def to_all(src, dst, ss, rs):
+    def slice_copy(src, dst, ss, rs, t, core):
+        return pltpu.make_async_remote_copy(
+            src_ref=src.at[t],
+            dst_ref=dst.at[m],
+            send_sem=ss,
+            recv_sem=rs,
+            device_id={"ctx": t * 2 + core, "head": x},
+            device_id_type=MESH,
+        )
+
+    def to_all(src, dst, ss, rs, lead=False):
         for n in range(CHIPS - 1):
             t = others(n)
-            pltpu.make_async_remote_copy(
-                src_ref=src.at[t],
-                dst_ref=dst.at[m],
-                send_sem=ss,
-                recv_sem=rs,
-                device_id=chip(t),
-                device_id_type=MESH,
-            ).start()
+            if lead and n == 0:
+                t = t * (1 - (m + CHIPS - 1) // CHIPS)
+            elif lead:
+                t = t + (1 - (t + CHIPS - 1) // CHIPS) * others(0)
+            slice_copy(src, dst, ss, rs, t, c).start()
 
     def bytes_of(buf, count, sem):
         part = buf.at[pl.ds(0, count)]
@@ -156,6 +164,14 @@
             t = CHIPS - 1 - n if reverse else n
             pb[i, t] = carry
             carry = fr[i, t] + keeps[t] * carry
+        if reverse:
+            g = i - GROUPS
+
+            @pl.when(c == 0)
+            def _():
+                for t in range(EARLY):
+                    slice_copy(pb.at[i], direct.at[g], dir_s.at[g], dir_r.at[g], t, 1).start()
+
         to_all(pb.at[i], sbuf.at[i], ret_s.at[i], ret_r.at[i])
         sbuf[i, pl.ds(m, 1)] = pb[i, pl.ds(m, 1)]
 
@@ -165,7 +181,11 @@
         away = part + weight * whole
         is_edge = c == edge
         snd[i] = jnp.where(is_edge, away, whole)
-        pair_copy(snd.at[i], stb.at[i], back_s.at[i], back_r.at[i]).start()
+
+        @pl.when(jnp.logical_or(edge == 0, jnp.logical_or(c == 1, m >= EARLY)))
+        def _():
+            pair_copy(snd.at[i], stb.at[i], back_s.at[i], back_r.at[i]).start()
+
         return jnp.where(is_edge, whole, away)
 
     loads[1].wait()
@@ -339,15 +359,30 @@
         tk[at, :] = dkp[h] + last_m[...] * nt(vh[h], state)
         tv[at, :] = dvp[h] + last_m[...] * nn(kh[h], state)
 
-    for g in range(GROUPS):
+    def own_last(g):
         own = split(GROUPS + g, 1, hodd[g], keep_odd).astype(bf16)
         for r in range(GH):
             last_of(c * HALF + g * GH + r, own[r * HEAD_DIM : (r + 1) * HEAD_DIM])
-    for g in range(GROUPS):
+
+    def other_last(g):
         i = GROUPS + g
-        pair_copy(snd.at[i], stb.at[i], back_s.at[i], back_r.at[i]).wait_recv()
+
+        @pl.when(jnp.logical_or(c == 0, m >= EARLY))
+        def _():
+            pair_copy(snd.at[i], stb.at[i], back_s.at[i], back_r.at[i]).wait_recv()
+
+        @pl.when(jnp.logical_and(c == 1, m < EARLY))
+        def _():
+            bytes_of(direct.at[g], CHIPS, dir_r.at[g])
+            stb[i] = direct[g].reshape(ROWS, HEAD_DIM)
+
         for r in range(GH):
             last_of(oc * HALF + g * GH + r, stb[i, rows_of(r)].astype(bf16))
+
+    own_last(0)
+    own_last(1)
+    other_last(0)
+    other_last(1)
 
     bytes_of(xb, len(peers), x_s)
     for swap in swaps:
@@ -355,8 +390,18 @@
     for g in range(GROUPS):
         firsts[g].wait_send()
         gives[g].wait_send()
+    for g in range(GROUPS):
+        pair_copy(snd.at[g], stb.at[g], back_s.at[g], back_r.at[g]).wait_send()
+
+        @pl.when(c == 0)
+        def _(g=g):
+            bytes_of(direct.at[g], EARLY, dir_s.at[g])
+
+        @pl.when(jnp.logical_or(c == 1, m >= EARLY))
+        def _(i=GROUPS + g):
+            pair_copy(snd.at[i], stb.at[i], back_s.at[i], back_r.at[i]).wait_send()
+
     for i in range(2 * GROUPS):
-        pair_copy(snd.at[i], stb.at[i], back_s.at[i], back_r.at[i]).wait_send()
         bytes_of(fr.at[i], CHIPS - 1, fwd_s.at[i])
         bytes_of(sbuf.at[i], CHIPS - 1, ret_s.at[i])
 
@@ -443,6 +488,7 @@
             slices,
             slices,
             slices,
+            V((GROUPS, CHIPS, SL, HEAD_DIM), f32),
             parts2,
             parts2,
             V((2 * XS, 8, HEAD_DIM), f32),
@@ -454,6 +500,8 @@
             D((N,)),
             D((N,)),
             D((N,)),
+            D((GROUPS,)),
+            D((GROUPS,)),
             D((N,)),
             D((N,)),
             D((3,)),

time: 52.2 us -> 50.8 us (0.973)
  Pallas kernels: 51.4 us -> 50 us
    pallas_call x1, Pallas kernels: 50.2 us -> 48.8 us  [local(): pl.pallas_call(kernel, out_shape=(out, flat, flat), in_specs=[hb] * 6, ou...]
where the time goes in v4:
time: 50.8 us; the launch traced here: 50.7 us
  Pallas kernels  50 us (98%)
  between operations  0.64 us (1%)
    pallas_call x1, Pallas kernels, local(): pl.pallas_call(kernel, out_shape=(out, flat, flat), in_specs=[hb] * 6, ou...  48.8 us
    pallas_call x1, Pallas kernels, local(): pl.pallas_call(finish, out_shape=(out, out, out), in_specs=[vm] * 3, out_...  1.21 us

profile of v4, /device:TPU:1, one launch (start us, length us, event | category | flops | bytes accessed | tf_op | source)
XLA Modules:
  0.0 50.7 jit_solution(5672880174589655744)
XLA Ops:
  0.6 48.8 %fused.1 = (bf16[256,8,128]{2,1,0:T(8,128)(2,1)S(1)}, f32[2048,128]{1,0:T(8,128)S(1)}, f32[2048,128]{1,0:T(8,128)S(1)}) custom-call(s32[4]{0:T(128)} %starts_in.1, f32[8,128]{1,0:T(8,128)} %gain_in.1, bf16[256,8,128]{2,1,0:T(8,128)(2,1)} %q_in.1, bf16[256,8,128]{2,1,0:T(8,128)(2,1)} %k_in.1, bf16[256,8,128]{2,1,0:T(8,128)(2,1)} %v_in.1, ...), custom_call_target="tpu_custom_call" | custom-call | flops 1400000000 | bytes 4000000 | tf_op jit(solution)/shard_map/fused/pallas_call | solution.py:444
  49.5 1.2 %finish.1 = (bf16[256,8,128]{2,1,0:T(8,128)(2,1)}, bf16[256,8,128]{2,1,0:T(8,128)(2,1)}, bf16[256,8,128]{2,1,0:T(8,128)(2,1)}) custom-call(bf16[256,8,128]{2,1,0:T(8,128)(2,1)S(1)} %get-tuple-element.6.oq, f32[2048,128]{1,0:T(8,128)S(1)} %get-tuple-element.7.tk, f32[2048,128]{1,0:T(8,128)S(1)} %get-tuple-element.8.tv), custom_call_target="tpu_custom_call" | custom-call | tf_op jit(solution)/shard_map/finish/pallas_call | solution.py:522

commit v5 on v4

--- a/solution.py
+++ b/solution.py
@@ -46,7 +46,7 @@
     starts, gain, raw, tmp, qh, kh, vh, sc, mask, mask_t, first_m, last_m, probs_t, dat, dkp, dvp,
     xin, xat, xsc, yin, ysc, yq, rq, yd, rd, xq, qft, st,
     sqp, crp, rr, co, keeps, tme, toth, tsib, hodd, pbuf, fr, pb, sbuf, direct, snd, stb, xb, tot,
-    in_sem, pair_s, pair_r, fwd_s, fwd_r, ret_s, ret_r, dir_s, dir_r, back_s, back_r, ex_s, ex_r, yd_s, yd_r, x_s, x_r,
+    in_sem, pair_s, pair_r, fwd_s, fwd_r, ret_s, ret_r, dir_s, dir_r, back_s, back_r, ex_s, ex_r, yd_s, yd_r, x_s, x_r, hello, go,
 ):
     b = lax.axis_index("ctx")
     x = lax.axis_index("head")
@@ -84,12 +84,24 @@
         if (d, e) != (0, 0)
     ]
     bar = pltpu.get_barrier_semaphore()
+
+    @pl.when(c == 1)
+    def _():
+        pl.semaphore_signal(bar, inc=1, device_id=sib, device_id_type=MESH)
+
     for n in range(CHIPS - 1):
-        pl.semaphore_signal(bar, inc=1, device_id=chip(others(n)), device_id_type=MESH)
-    for peer in peers:
-        pl.semaphore_signal(bar, inc=1, device_id=peer, device_id_type=MESH)
+        far = {"ctx": others(n) * 2 + 1, "head": x}
+        pl.semaphore_signal(bar, inc=1, device_id=far, device_id_type=MESH)
+    for d in (2, 1, 3):
+        side = {"ctx": m * 2 + 1, "head": lax.rem(x + d, XS)}
+        pl.semaphore_signal(bar, inc=1, device_id=side, device_id_type=MESH)
     for load in loads:
         load.start()
+
+    @pl.when(c == 0)
+    def _():
+        pl.semaphore_wait(bar, 1)
+        pl.semaphore_signal(hello, inc=1, device_id=sib, device_id_type=MESH)
 
     loads[0].wait()
     sv = [starts[n] for n in range(4)]
@@ -152,8 +164,7 @@
     def rows_of(r):
         return pl.ds(r * HEAD_DIM, HEAD_DIM)
 
-    def forward(i, p):
-        pbuf[i] = p.reshape(CHIPS, SL, HEAD_DIM)
+    def forward(i):
         to_all(pbuf.at[i], fr.at[i], fwd_s.at[i], fwd_r.at[i])
         fr[i, pl.ds(m, 1)] = pbuf[i, pl.ds(m, 1)]
 
@@ -196,22 +207,38 @@
     def tail_of(h):
         return tn((kh[h].astype(f32) * last_m[...]).astype(bf16), vh[h])
 
+    firsts = [pair_copy(toth.at[g], tsib.at[g], pair_s.at[g], pair_r.at[g]) for g in range(GROUPS)]
     for g in range(GROUPS):
         for r in range(GH):
             toth[g, rows_of(r)] = tail_of(oc * HALF + g * GH + r)
+        if g == 0:
+
+            @pl.when(c == 1)
+            def _():
+                pl.semaphore_wait(hello, 1)
+
+        firsts[g].start()
     for g in range(GROUPS):
         for r in range(GH):
             tme[g, rows_of(r)] = tail_of(c * HALF + g * GH + r)
-    pl.semaphore_wait(bar, CHIPS - 1 + len(peers))
     one = jnp.ones((), f32)
     w_me = jnp.where(c == 0, keep_odd, one)
     w_sib = jnp.where(c == 0, one, keep_odd)
-    firsts = [pair_copy(toth.at[g], tsib.at[g], pair_s.at[g], pair_r.at[g]) for g in range(GROUPS)]
-    for g in range(GROUPS):
-        firsts[g].start()
     for g in range(GROUPS):
         firsts[g].wait_recv()
-        forward(g, tme[g] * w_me + tsib[g] * w_sib)
+        pbuf[g] = (tme[g] * w_me + tsib[g] * w_sib).reshape(CHIPS, SL, HEAD_DIM)
+
+    @pl.when(c == 1)
+    def _():
+        pl.semaphore_wait(bar, 2 * (CHIPS - 1) + 2 * (XS - 1))
+        pl.semaphore_signal(go, inc=1, device_id=sib, device_id_type=MESH)
+
+    @pl.when(c == 0)
+    def _():
+        pl.semaphore_wait(go, 1)
+
+    for g in range(GROUPS):
+        forward(g)
 
     chip_row = lax.broadcasted_iota(jnp.int32, (CHIPS, SL, HEAD_DIM), 0)
     keeps[...] = keep(chip_row * (2 * TOK), 2 * TOK)
@@ -330,7 +357,8 @@
             odd = jnp.where(c == 0, pair[1], pair[0])
             hodd[g, rows_of(r)] = odd
             parts.append(even + keep_even * odd)
-        forward(GROUPS + g, jnp.concatenate(parts, axis=0))
+        pbuf[GROUPS + g] = jnp.concatenate(parts, axis=0).reshape(CHIPS, SL, HEAD_DIM)
+        forward(GROUPS + g)
         gives[g].start()
 
     def near_bwd(h, state):
@@ -510,6 +538,8 @@
             D((GROUPS,)),
             D,
             D,
+            pltpu.SemaphoreType.REGULAR,
+            pltpu.SemaphoreType.REGULAR,
         ],
         compiler_params=pltpu.CompilerParams(
             collective_id=0, has_side_effects=True, vmem_limit_bytes=32 * 2**20

time: 50.8 us -> 50.6 us (level)
  Pallas kernels: 50 us -> 49.3 us
    pallas_call x1, Pallas kernels: 48.8 us -> 48.1 us  [local(): pl.pallas_call(kernel, out_shape=(out, flat, flat), in_specs=[hb] * 6, ou...]
where the time goes in v5:
time: 50.6 us; the launch traced here: 50 us
  Pallas kernels  49.3 us (97%)
  between operations  0.64 us (1%)
    pallas_call x1, Pallas kernels, local(): pl.pallas_call(kernel, out_shape=(out, flat, flat), in_specs=[hb] * 6, ou...  48.1 us
    pallas_call x1, Pallas kernels, local(): pl.pallas_call(finish, out_shape=(out, out, out), in_specs=[vm] * 3, out_...  1.21 us

profile of v5, /device:TPU:1, one launch (start us, length us, event | category | flops | bytes accessed | tf_op | source)
XLA Modules:
  0.0 50.0 jit_solution(1347976195052747104)
XLA Ops:
  0.6 48.1 %fused.1 = (bf16[256,8,128]{2,1,0:T(8,128)(2,1)S(1)}, f32[2048,128]{1,0:T(8,128)S(1)}, f32[2048,128]{1,0:T(8,128)S(1)}) custom-call(s32[4]{0:T(128)} %starts_in.1, f32[8,128]{1,0:T(8,128)} %gain_in.1, bf16[256,8,128]{2,1,0:T(8,128)(2,1)} %q_in.1, bf16[256,8,128]{2,1,0:T(8,128)(2,1)} %k_in.1, bf16[256,8,128]{2,1,0:T(8,128)(2,1)} %v_in.1, ...), custom_call_target="tpu_custom_call" | custom-call | flops 1400000000 | bytes 4000000 | tf_op jit(solution)/shard_map/fused/pallas_call | solution.py:472
  48.8 1.2 %finish.1 = (bf16[256,8,128]{2,1,0:T(8,128)(2,1)}, bf16[256,8,128]{2,1,0:T(8,128)(2,1)}, bf16[256,8,128]{2,1,0:T(8,128)(2,1)}) custom-call(bf16[256,8,128]{2,1,0:T(8,128)(2,1)S(1)} %get-tuple-element.6.oq, f32[2048,128]{1,0:T(8,128)S(1)} %get-tuple-element.7.tk, f32[2048,128]{1,0:T(8,128)S(1)} %get-tuple-element.8.tv), custom_call_target="tpu_custom_call" | custom-call | tf_op jit(solution)/shard_map/finish/pallas_call | solution.py:552

commit v6 on v5

--- a/solution.py
+++ b/solution.py
@@ -22,8 +22,15 @@
 PIECES = 4
 FAR = sorted(
     ((dz, dy) for dz in range(ZS) for dy in range(YS) if dz or dy),
-    key=lambda o: -(min(o[0], ZS - o[0]) + min(o[1], YS - o[1])),
+    key=lambda o: (-min(o[0], ZS - o[0]), -min(o[1], YS - o[1])),
 )
+def reach(o):
+    z = min(o[0], ZS - o[0])
+    y = min(o[1], YS - o[1])
+    return 0.43 * z + 0.15 * y + (0.55 if z and y else 0.0)
+
+
+ORDER = sorted(FAR, key=lambda o: -reach(o))
 MESH = pl.DeviceIdType.MESH
 f32 = jnp.float32
 bf16 = jnp.bfloat16
@@ -74,8 +81,8 @@
         )
     ]
 
-    def others(n):
-        return lax.rem(mz + FAR[n][0], ZS) * YS + lax.rem(my + FAR[n][1], YS)
+    def others(n, order=FAR):
+        return lax.rem(mz + order[n][0], ZS) * YS + lax.rem(my + order[n][1], YS)
 
     peers = [
         {"ctx": m * 2 + lax.rem(c + e, 2), "head": lax.rem(x + d, XS)}
@@ -148,14 +155,11 @@
             device_id_type=MESH,
         )
 
-    def to_all(src, dst, ss, rs, lead=False):
-        for n in range(CHIPS - 1):
-            t = others(n)
-            if lead and n == 0:
-                t = t * (1 - (m + CHIPS - 1) // CHIPS)
-            elif lead:
-                t = t + (1 - (t + CHIPS - 1) // CHIPS) * others(0)
-            slice_copy(src, dst, ss, rs, t, c).start()
+    def send_out(out, groups):
+        src, dst, ss, rs = out
+        for i in groups:
+            for n in range(CHIPS - 1):
+                slice_copy(src.at[i], dst.at[i], ss.at[i], rs.at[i], others(n, ORDER), c).start()
 
     def bytes_of(buf, count, sem):
         part = buf.at[pl.ds(0, count)]
@@ -164,9 +168,8 @@
     def rows_of(r):
         return pl.ds(r * HEAD_DIM, HEAD_DIM)
 
-    def forward(i):
-        to_all(pbuf.at[i], fr.at[i], fwd_s.at[i], fwd_r.at[i])
-        fr[i, pl.ds(m, 1)] = pbuf[i, pl.ds(m, 1)]
+    going = (pbuf, fr, fwd_s, fwd_r)
+    coming = (pb, sbuf, ret_s, ret_r)
 
     def turn(i, reverse):
         bytes_of(fr.at[i], CHIPS - 1, fwd_r.at[i])
@@ -183,7 +186,7 @@
                 for t in range(EARLY):
                     slice_copy(pb.at[i], direct.at[g], dir_s.at[g], dir_r.at[g], t, 1).start()
 
-        to_all(pb.at[i], sbuf.at[i], ret_s.at[i], ret_r.at[i])
+        send_out(coming, (i,))
         sbuf[i, pl.ds(m, 1)] = pb[i, pl.ds(m, 1)]
 
     def split(i, edge, part, weight):
@@ -237,9 +240,11 @@
     def _():
         pl.semaphore_wait(go, 1)
 
-    for g in range(GROUPS):
-        forward(g)
-
+    first = range(GROUPS)
+    second = range(GROUPS, 2 * GROUPS)
+    send_out(going, first)
+    for g in first:
+        fr[g, pl.ds(m, 1)] = pbuf[g, pl.ds(m, 1)]
     chip_row = lax.broadcasted_iota(jnp.int32, (CHIPS, SL, HEAD_DIM), 0)
     keeps[...] = keep(chip_row * (2 * TOK), 2 * TOK)
     loads[3].wait()
@@ -358,7 +363,8 @@
             hodd[g, rows_of(r)] = odd
             parts.append(even + keep_even * odd)
         pbuf[GROUPS + g] = jnp.concatenate(parts, axis=0).reshape(CHIPS, SL, HEAD_DIM)
-        forward(GROUPS + g)
+        fr[GROUPS + g, pl.ds(m, 1)] = pbuf[GROUPS + g, pl.ds(m, 1)]
+        send_out(going, (GROUPS + g,))
         gives[g].start()
 
     def near_bwd(h, state):
@@ -371,8 +377,8 @@
 
     for r in range(HALF):
         near_bwd(c * HALF + r, st[0, r])
-    for g in range(GROUPS):
-        turn(GROUPS + g, True)
+    for i in second:
+        turn(i, True)
     for g in range(GROUPS):
         pair_copy(snd.at[g], stb.at[g], back_s.at[g], back_r.at[g]).wait_recv()
         gives[g].wait_recv()

time: 50.6 us -> 50 us (0.988)
  no operation moved by 1% of the time
where the time goes in v6:
time: 50 us; the launch traced here: 49.7 us
  Pallas kernels  49.1 us (98%)
  between operations  0.64 us (1%)
    pallas_call x1, Pallas kernels, local(): pl.pallas_call(kernel, out_shape=(out, flat, flat), in_specs=[hb] * 6, ou...  47.8 us
    pallas_call x1, Pallas kernels, local(): pl.pallas_call(finish, out_shape=(out, out, out), in_specs=[vm] * 3, out_...  1.21 us

profile of v6, /device:TPU:1, one launch (start us, length us, event | category | flops | bytes accessed | tf_op | source)
XLA Modules:
  0.0 49.7 jit_solution(16232596932680131505)
XLA Ops:
  0.6 47.8 %fused.1 = (bf16[256,8,128]{2,1,0:T(8,128)(2,1)S(1)}, f32[2048,128]{1,0:T(8,128)S(1)}, f32[2048,128]{1,0:T(8,128)S(1)}) custom-call(s32[4]{0:T(128)} %starts_in.1, f32[8,128]{1,0:T(8,128)} %gain_in.1, bf16[256,8,128]{2,1,0:T(8,128)(2,1)} %q_in.1, bf16[256,8,128]{2,1,0:T(8,128)(2,1)} %k_in.1, bf16[256,8,128]{2,1,0:T(8,128)(2,1)} %v_in.1, ...), custom_call_target="tpu_custom_call" | custom-call | flops 1400000000 | bytes 4000000 | tf_op jit(solution)/shard_map/fused/pallas_call | solution.py:478
  48.5 1.2 %finish.1 = (bf16[256,8,128]{2,1,0:T(8,128)(2,1)}, bf16[256,8,128]{2,1,0:T(8,128)(2,1)}, bf16[256,8,128]{2,1,0:T(8,128)(2,1)}) custom-call(bf16[256,8,128]{2,1,0:T(8,128)(2,1)S(1)} %get-tuple-element.6.oq, f32[2048,128]{1,0:T(8,128)S(1)} %get-tuple-element.7.tk, f32[2048,128]{1,0:T(8,128)S(1)} %get-tuple-element.8.tv), custom_call_target="tpu_custom_call" | custom-call | tf_op jit(solution)/shard_map/finish/pallas_call | solution.py:558

commit v7 on v6

--- a/solution.py
+++ b/solution.py
@@ -27,7 +27,7 @@
 def reach(o):
     z = min(o[0], ZS - o[0])
     y = min(o[1], YS - o[1])
-    return 0.43 * z + 0.15 * y + (0.55 if z and y else 0.0)
+    return 0.43 * z + 0.4 * y + (0.55 if z and y else 0.0)
 
 
 ORDER = sorted(FAR, key=lambda o: -reach(o))
@@ -50,7 +50,7 @@
 
 def kernel(
     starts_in, gain_in, q_in, k_in, v_in, g_in, oq, tk, tv,
-    starts, gain, raw, tmp, qh, kh, vh, sc, mask, mask_t, first_m, last_m, probs_t, dat, dkp, dvp,
+    starts, gain, raw, tmp, qh, kh, vh, sc, mask, mask_t, first_m, last_m, probs_t, dat, dqp, dkp, dvp,
     xin, xat, xsc, yin, ysc, yq, rq, yd, rd, xq, qft, st,
     sqp, crp, rr, co, keeps, tme, toth, tsib, hodd, pbuf, fr, pb, sbuf, direct, snd, stb, xb, tot,
     in_sem, pair_s, pair_r, fwd_s, fwd_r, ret_s, ret_r, dir_s, dir_r, back_s, back_r, ex_s, ex_r, yd_s, yd_r, x_s, x_r, hello, go,
@@ -97,7 +97,7 @@
         pl.semaphore_signal(bar, inc=1, device_id=sib, device_id_type=MESH)
 
     for n in range(CHIPS - 1):
-        far = {"ctx": others(n) * 2 + 1, "head": x}
+        far = {"ctx": others(n, ORDER) * 2 + 1, "head": x}
         pl.semaphore_signal(bar, inc=1, device_id=far, device_id_type=MESH)
     for d in (2, 1, 3):
         side = {"ctx": m * 2 + 1, "head": lax.rem(x + d, XS)}
@@ -371,7 +371,7 @@
         dp = (nt(dat[h], vh[h]) * mask[...]).astype(bf16)
         dpt = (nt(vh[h], dat[h]) * mask_t[...]).astype(bf16)
         dq = nn(dp, kh[h]) + first_m[...] * nt(dat[h], state)
-        tmp[pl.ds(h, TOK, stride=LH), :] = dq
+        dqp[h] = dq
         dkp[h] = nn(dpt, qh[h])
         dvp[h] = nn(probs_t[h], dat[h])
 
@@ -386,6 +386,8 @@
             h = oc * HALF + g * GH + r
             dat[h] = rd[g, r].astype(bf16)
             near_bwd(h, stb[g, rows_of(r)].astype(bf16))
+    for h in range(LH):
+        tmp[pl.ds(h, TOK, stride=LH), :] = dqp[h]
     oq[...] = tmp[...].reshape(TOK, LH, HEAD_DIM).astype(bf16)
 
     def last_of(h, state):
@@ -395,8 +397,12 @@
 
     def own_last(g):
         own = split(GROUPS + g, 1, hodd[g], keep_odd).astype(bf16)
-        for r in range(GH):
-            last_of(c * HALF + g * GH + r, own[r * HEAD_DIM : (r + 1) * HEAD_DIM])
+        for core in range(2):
+
+            @pl.when(c == core)
+            def _(core=core):
+                for r in range(GH):
+                    last_of(core * HALF + g * GH + r, own[r * HEAD_DIM : (r + 1) * HEAD_DIM])
 
     def other_last(g):
         i = GROUPS + g
@@ -410,8 +416,12 @@
             bytes_of(direct.at[g], CHIPS, dir_r.at[g])
             stb[i] = direct[g].reshape(ROWS, HEAD_DIM)
 
-        for r in range(GH):
-            last_of(oc * HALF + g * GH + r, stb[i, rows_of(r)].astype(bf16))
+        for core in range(2):
+
+            @pl.when(oc == core)
+            def _(core=core):
+                for r in range(GH):
+                    last_of(core * HALF + g * GH + r, stb[i, rows_of(r)].astype(bf16))
 
     own_last(0)
     own_last(1)
@@ -495,6 +505,7 @@
             cols,
             V((LH, TOK, TOK), bf16),
             heads16,
+            heads32,
             heads32,
             heads32,
             both32,

time: 50 us -> 49.9 us (level)
  no operation moved by 1% of the time
where the time goes in v7:
time: 49.9 us; the launch traced here: 49.8 us
  Pallas kernels  49.1 us (98%)
  between operations  0.64 us (1%)
    pallas_call x1, Pallas kernels, local(): pl.pallas_call(kernel, out_shape=(out, flat, flat), in_specs=[hb] * 6, ou...  47.9 us
    pallas_call x1, Pallas kernels, local(): pl.pallas_call(finish, out_shape=(out, out, out), in_specs=[vm] * 3, out_...  1.21 us

profile of v7, /device:TPU:1, one launch (start us, length us, event | category | flops | bytes accessed | tf_op | source)
XLA Modules:
  0.0 49.8 jit_solution(16745421533088282800)
XLA Ops:
  0.6 47.9 %fused.1 = (bf16[256,8,128]{2,1,0:T(8,128)(2,1)S(1)}, f32[2048,128]{1,0:T(8,128)S(1)}, f32[2048,128]{1,0:T(8,128)S(1)}) custom-call(s32[4]{0:T(128)} %starts_in.1, f32[8,128]{1,0:T(8,128)} %gain_in.1, bf16[256,8,128]{2,1,0:T(8,128)(2,1)} %q_in.1, bf16[256,8,128]{2,1,0:T(8,128)(2,1)} %k_in.1, bf16[256,8,128]{2,1,0:T(8,128)(2,1)} %v_in.1, ...), custom_call_target="tpu_custom_call" | custom-call | flops 1400000000 | bytes 4000000 | tf_op jit(solution)/shard_map/fused/pallas_call | solution.py:488
  48.6 1.2 %finish.1 = (bf16[256,8,128]{2,1,0:T(8,128)(2,1)}, bf16[256,8,128]{2,1,0:T(8,128)(2,1)}, bf16[256,8,128]{2,1,0:T(8,128)(2,1)}) custom-call(bf16[256,8,128]{2,1,0:T(8,128)(2,1)S(1)} %get-tuple-element.6.oq, f32[2048,128]{1,0:T(8,128)S(1)} %get-tuple-element.7.tk, f32[2048,128]{1,0:T(8,128)S(1)} %get-tuple-element.8.tv), custom_call_target="tpu_custom_call" | custom-call | tf_op jit(solution)/shard_map/finish/pallas_call | solution.py:569
